TPU v7x, 256 devices: a whole 4x4x8 slice. The times are simulated.
256 devices in a mesh: chrom: 128 (over z, x_lo, y, core), chan: 2 (over x_hi).
Axes of the slice: x: 4 (x_hi: 2, x_lo: 2; x = x_hi * 2 + x_lo), y: 4, z: 8, core: 2. Of those that a mesh axis runs over, the one named last changes fastest.
Arguments:
- embeddings: bfloat16 [8192, 512], P('chrom', 'chan'), may hold values from -6 to 6
- w_left: bfloat16 [512, 32], P(None, 'chan'), may hold values from -0.25 to 0.25
- w_right: bfloat16 [512, 32], P(None, 'chan'), may hold values from -0.25 to 0.25
- first_conv_weight: bfloat16 [32, 3, 3, 16], P('chan'), may hold values from -0.5 to 0.5
- second_conv_weight: bfloat16 [32, 3, 3, 16], P('chan'), may hold values from -0.5 to 0.5
- head_weight: float32 [32], P('chan'), may hold values from -1 to 1
- cotangent: bfloat16 [8192, 512], P('chrom'), may hold values from -6 to 6
- dilations: int32 [2], replicated, may hold values from 1 to 8, as said below
- chrom_ends: int32 [8], replicated, may hold values from 1 to 8192, as said below
Outputs:
- contacts: float32 [8192, 512], P('chrom')
- emb_grad: bfloat16 [8192, 512], P('chrom', 'chan')
- left_weight_grad: float32 [512, 32], P(None, 'chan')
- right_weight_grad: float32 [512, 32], P(None, 'chan')
- first_conv_grad: float32 [32, 3, 3, 16], P('chan')
- second_conv_grad: float32 [32, 3, 3, 16], P('chan')
- head_grad: float32 [32], P('chan')
Inputs may be any that keep to these rules, and one draw needn't show every extreme that they name: `dilations`: one of the two convolutions has dilation 8, the other a smaller one. `chrom_ends`: strictly increasing; the last entry equals 8192.
All inputs are finite; a program needn't handle non-finite values.
Results may differ from a plain program's by a relative error of at most 0.015.
Values may be sent and summed in bfloat16 or wider, within the bound.
A program may use at most 64 MiB of HBM per device.

v0:
```python
import math

import jax
import jax.numpy as jnp
from jax import lax
from jax.sharding import PartitionSpec as P

OFF = 512
LARGEST_DILATION = 8


INV_ROOT_TWO = 0.7071067811865476
INV_ROOT_TWO_PI = 0.3989422804014327


def from_behind(block, axis, distance):
    devices = range(lax.axis_size(axis))
    route = [(i - distance, i) for i in devices if i - distance in devices]
    return lax.ppermute(block, axis, route)


def with_halo(block, sides, width):
    for axis, dim in sides:
        count = lax.axis_size(axis)
        forward = [(i, i + 1) for i in range(count - 1)]
        backward = [(target, source) for source, target in forward]
        low = lax.ppermute(
            lax.slice_in_dim(block, block.shape[dim] - width, None, axis=dim), axis, forward
        )
        high = lax.ppermute(lax.slice_in_dim(block, 0, width, axis=dim), axis, backward)
        block = jnp.concatenate([low, block, high], axis=dim)
    return block


def gelu_value(values):
    return values * 0.5 * (1.0 + lax.erf(values * INV_ROOT_TWO))


def gelu_slope(values):
    return (
        0.5 * (1.0 + lax.erf(values * INV_ROOT_TWO))
        + values * jnp.exp(-0.5 * values * values) * INV_ROOT_TWO_PI
    )


def chrom_index(position, chrom_ends):
    return jnp.sum((chrom_ends <= position[..., None]).astype(jnp.int32), axis=-1)


def band_valid(first_row, row_count, chrom_ends, bin_total):
    row_pos = first_row + jnp.arange(row_count, dtype=jnp.int32)[:, None]
    col_pos = row_pos + jnp.arange(OFF, dtype=jnp.int32)[None, :]
    same = chrom_index(row_pos, chrom_ends) == chrom_index(col_pos, chrom_ends)
    valid_mask = (row_pos >= 0) & (col_pos < bin_total) & same
    return valid_mask.astype(jnp.float32)


def side_pad(field):
    return jnp.pad(field, ((0, 0), (0, 0), (2 * LARGEST_DILATION, 2 * LARGEST_DILATION)))


def window(padded, top_row, side_col, row_count):
    starts = (jnp.int32(0), jnp.asarray(top_row), jnp.asarray(side_col))
    return lax.dynamic_slice(padded, starts, (padded.shape[0], row_count, OFF))


def apply_convolution(weight, rim_field, dilation, base_row, row_count):
    padded = side_pad(rim_field)
    channels = weight.shape[0]
    result = jnp.zeros((channels, row_count, OFF), jnp.float32)
    for row_tap, a in enumerate((-1, 0, 1)):
        stacked = jnp.concatenate(
            [
                window(
                    padded,
                    base_row + a * dilation,
                    2 * LARGEST_DILATION + (b - a) * dilation,
                    row_count,
                )
                for b in (-1, 0, 1)
            ],
            axis=0,
        )
        tap_matrix = weight[:, row_tap].reshape(channels, 3 * channels)
        result = result + jnp.einsum(
            "ot,tik->oik", tap_matrix, stacked, preferred_element_type=jnp.float32
        )
    return result


def convolution_transpose(weight, rim_grad, dilation, base_row, row_count):
    padded = side_pad(rim_grad)
    channels = weight.shape[0]
    result = jnp.zeros((channels, row_count, OFF), jnp.float32)
    for row_tap, a in enumerate((-1, 0, 1)):
        stacked = jnp.concatenate(
            [
                window(
                    padded,
                    base_row - a * dilation,
                    2 * LARGEST_DILATION - (b - a) * dilation,
                    row_count,
                )
                for b in (-1, 0, 1)
            ],
            axis=0,
        )
        tap_matrix = jnp.transpose(weight[:, row_tap], (1, 0, 2)).reshape(3 * channels, channels)
        result = result + jnp.einsum(
            "tc,tik->cik", tap_matrix, stacked, preferred_element_type=jnp.float32
        )
    return result


def convolution_weight_gradient(grad_out, rim_field, dilation, base_row, row_count):
    padded = side_pad(rim_field)
    channels = grad_out.shape[0]
    rows_out = []
    for a in (-1, 0, 1):
        stacked = jnp.concatenate(
            [
                window(
                    padded,
                    base_row + a * dilation,
                    2 * LARGEST_DILATION + (b - a) * dilation,
                    row_count,
                )
                for b in (-1, 0, 1)
            ],
            axis=0,
        )
        product = jnp.einsum("oik,tik->ot", grad_out, stacked, preferred_element_type=jnp.float32)
        rows_out.append(product.reshape(channels, 3, channels))
    return jnp.stack(rows_out, axis=1)


def skew_rows(extended, row_count):
    channels, length = extended.shape
    tiled = jnp.broadcast_to(extended[:, None, :], (channels, row_count, length)).reshape(
        channels, row_count * length
    )
    padded = jnp.pad(tiled, ((0, 0), (0, row_count)))
    return padded.reshape(channels, row_count, length + 1)[:, :, :OFF]


def unskew_rows(banded, row_count):
    channels = banded.shape[0]
    length = row_count + OFF
    padded = jnp.pad(banded, ((0, 0), (0, 0), (0, length + 1 - OFF)))
    flat = padded.reshape(channels, row_count * (length + 1))[:, : row_count * length]
    return jnp.sum(flat.reshape(channels, row_count, length), axis=1)


def on_device(
    embeddings,
    w_left,
    w_right,
    first_conv_weight,
    second_conv_weight,
    head_weight,
    cotangent,
    dilations,
    chrom_ends,
):
    count_of_bins = embeddings.shape[0]
    devices = lax.axis_size("chrom")
    bin_total = count_of_bins * devices
    reach_devices = OFF // count_of_bins
    row_start = lax.axis_index("chrom") * count_of_bins
    first_dilation = dilations[0]
    second_dilation = dilations[1]
    full_emb = lax.all_gather(embeddings, "chan", axis=1, tiled=True)
    left_proj = jnp.dot(full_emb, w_left, preferred_element_type=jnp.float32)
    right_proj = jnp.dot(full_emb, w_right, preferred_element_type=jnp.float32)
    right_pieces = [right_proj]
    for distance in range(1, reach_devices + 1):
        right_pieces.append(from_behind(right_proj, "chrom", -distance))
    right_ext = jnp.concatenate(right_pieces, axis=0)
    valid_mask = band_valid(row_start, count_of_bins, chrom_ends, bin_total)
    outer_valid = band_valid(
        row_start - LARGEST_DILATION, count_of_bins + 2 * LARGEST_DILATION, chrom_ends, bin_total
    )
    left_cols = left_proj.T[:, :, None]
    right_band = skew_rows(right_ext.T, count_of_bins)
    pair_feature_map = (valid_mask * left_cols * right_band).astype(jnp.bfloat16)
    pair_border = with_halo(pair_feature_map, (("chrom", 1),), LARGEST_DILATION)
    first_output_field = valid_mask * apply_convolution(
        first_conv_weight, pair_border, first_dilation, LARGEST_DILATION, count_of_bins
    )
    hidden_own = gelu_value(first_output_field).astype(jnp.bfloat16)
    hidden_border = with_halo(hidden_own, (("chrom", 1),), LARGEST_DILATION)
    second_output_field = valid_mask * apply_convolution(
        second_conv_weight, hidden_border, second_dilation, LARGEST_DILATION, count_of_bins
    )
    field = pair_feature_map.astype(jnp.float32) + second_output_field
    contact_part = jnp.einsum("c,cik->ik", head_weight, field)
    contacts = lax.psum(contact_part.astype(jnp.bfloat16), "chan").astype(jnp.float32)
    grad_rim = with_halo(cotangent, (("chrom", 0),), LARGEST_DILATION)
    second_border_gradient = (
        head_weight[:, None, None] * (outer_valid * grad_rim.astype(jnp.float32))[None]
    ).astype(jnp.bfloat16)
    hidden_gradient = convolution_transpose(
        second_conv_weight, second_border_gradient, second_dilation, LARGEST_DILATION, count_of_bins
    )
    first_output_gradient = (valid_mask * gelu_slope(first_output_field) * hidden_gradient).astype(
        jnp.bfloat16
    )
    second_weight_gradient = convolution_weight_gradient(
        second_border_gradient[:, LARGEST_DILATION : LARGEST_DILATION + count_of_bins],
        hidden_border,
        second_dilation,
        LARGEST_DILATION,
        count_of_bins,
    )
    first_border_gradient = with_halo(first_output_gradient, (("chrom", 1),), LARGEST_DILATION)
    input_gradient = cotangent.astype(jnp.float32)
    pair_gradient = head_weight[:, None, None] * input_gradient[None] + convolution_transpose(
        first_conv_weight, first_border_gradient, first_dilation, LARGEST_DILATION, count_of_bins
    )
    first_weight_gradient = convolution_weight_gradient(
        first_output_gradient, pair_border, first_dilation, LARGEST_DILATION, count_of_bins
    )
    head_part = jnp.sum(field * input_gradient[None], axis=(1, 2))
    left_grad = jnp.sum(valid_mask * right_band * pair_gradient, axis=2).T
    spread = valid_mask * left_cols * pair_gradient
    right_terms = unskew_rows(spread, count_of_bins)
    right_grad_cols = right_terms[:, :count_of_bins]
    for distance in range(1, reach_devices + 1):
        sent_piece = right_terms[:, distance * count_of_bins : (distance + 1) * count_of_bins]
        right_grad_cols = right_grad_cols + from_behind(sent_piece, "chrom", distance)
    left_low = left_grad.astype(jnp.bfloat16)
    right_low = right_grad_cols.T.astype(jnp.bfloat16)
    emb_part = jnp.dot(left_low, w_left.T, preferred_element_type=jnp.float32) + jnp.dot(
        right_low, w_right.T, preferred_element_type=jnp.float32
    )
    emb_grad = lax.psum_scatter(
        emb_part.astype(jnp.bfloat16), "chan", scatter_dimension=1, tiled=True
    )
    contract_rows = (((0,), (0,)), ((), ()))
    left_wpart = lax.dot_general(
        full_emb, left_low, contract_rows, preferred_element_type=jnp.float32
    )
    right_wpart = lax.dot_general(
        full_emb, right_low, contract_rows, preferred_element_type=jnp.float32
    )
    summed = lax.psum(
        (left_wpart, right_wpart, first_weight_gradient, second_weight_gradient, head_part), "chrom"
    )
    scale = 1.0 / math.sqrt(bin_total * OFF)
    return (
        contacts,
        emb_grad,
        summed[0] * scale,
        summed[1] * scale,
        summed[2] * scale,
        summed[3] * scale,
        summed[4] * scale,
    )


def solution(mesh):
    in_specs = (
        P("chrom", "chan"),
        P(None, "chan"),
        P(None, "chan"),
        P("chan", None, None, None),
        P("chan", None, None, None),
        P("chan"),
        P("chrom", None),
        P(),
        P(),
    )
    out_specs = (
        P("chrom", None),
        P("chrom", "chan"),
        P(None, "chan"),
        P(None, "chan"),
        P("chan", None, None, None),
        P("chan", None, None, None),
        P("chan"),
    )
    return jax.shard_map(
        on_device, mesh=mesh, in_specs=in_specs, out_specs=out_specs, check_vma=False
    )
```

profile of v0, /device:TPU:1, one launch (start us, length us, event | category | flops | bytes accessed | tf_op | source)
XLA Modules:
  0.0 1228.7 jit_solution(8260016891174936031)
XLA Ops:
  7.2 5.8 all_gather.3
  48.2 5.7 collective-permute-start
  58.0 4.2 collective-permute-start.12
  62.2 1.9 collective-permute-start.13
  64.4 2.3 reshape.440
  68.5 3.6 reshape.441
  75.4 3.6 collective-permute-start.8
  79.0 2.4 collective-permute-start.9
  82.7 4.8 pad_dynamic-slice_fusion.2
  87.5 1.9 fusion.1
  89.5 2.1 fusion.7
  92.5 6.3 constant_dynamic-slice_fusion.18
  110.8 3.5 collective-permute-start.10
  114.4 1.9 collective-permute-start.11
  120.6 3.6 collective-permute-start.14
  124.3 1.9 collective-permute-start.15
  127.6 2.2 select_maximum_fusion.2
  129.9 5.3 constant_dynamic-slice_fusion.10
  144.6 5.3 constant_dynamic-slice_fusion.2
  151.9 2.1 multiply_multiply_fusion.1
  155.6 2.5 reshape.448
  158.1 3.3 slice.126
  161.4 2.6 reshape.449
  164.3 3.6 collective-permute-start.16
  168.0 12.1 collective-permute-start.23
  180.1 14.8 %collective-permute-start.22 = (f32[16,64]{1,0:T(8,128)S(1)}, f32[16,64]{1,0:T(8,128)S(1)}, u32[]{:S(2)}, u32[]{:S(2)}) collective-permute-start(f32[16,64]{1,0:T(8,128)S(1)} %get-tuple-element.78), channel_id=1, source_target_pairs={{0,14},{2,16},{4,18},{6,20},{8,22},{10,24},{12,26},{14,28},{16,30}... | collective-permute-start | bytes 12296 | tf_op jit(solution)/shard_map/ppermute | solution.py:19
  196.7 4.0 collective-permute-start.21
  202.0 11.0 collective-permute-start.19
  214.4 4.0 collective-permute-start.17
  220.8 17.8 %all-reduce.10.cloned.1.call-done = bf16[64,512]{1,0:T(8,128)(2,1)} async-done(((bf16[64,512]{1,0:T(8,128)(2,1)}), bf16[64,512]{1,0:T(8,128)(2,1)}) %all-reduce.10.cloned.1.call-update) | async-done | bytes 65552 | tf_op jit(solution)/shard_map/psum | solution.py:197
  240.2 963.0 %all-reduce.12.cloned.1.call-done = (f32[512,16]{0,1:T(8,128)}, f32[512,16]{0,1:T(8,128)}, f32[16,3,3,16]{3,2,0,1:T(4,128)}, f32[16,3,3,16]{3,2,0,1:T(4,128)}, f32[16]{0:T(128)}) async-done(((f32[512,16]{0,1:T(8,128)}, f32[512,16]{0,1:T(8,128)}, f32[16,3,3,16]{3,2,0,1:T(4,128)}, f32[16,3,3,16]{3,2,0,1:T(4,128)}, f32[16]{0:T(128)}), (f32[512,16]{0,1:T(8,128)}, f32[512,16]{0,1:T(8,128)}, ...) | async-done | bytes 84048 | tf_op jit(solution)/shard_map/psum | solution.py:246
  1208.0 13.9 %reduce-scatter.2.cloned.1.call-done = bf16[64,256]{1,0:T(8,128)(2,1)} async-done(((bf16[64,512]{1,0:T(8,128)(2,1)}), bf16[64,256]{1,0:T(8,128)(2,1)}) %reduce-scatter.2.cloned.1.call-update) | async-done | bytes 32784 | tf_op jit(solution)/shard_map/reduce_scatter | solution.py:236
  (205 shorter events, 76.2 us)
Async XLA Ops:
  7.2 231.5 %all-reduce.10.cloned.1.call-start = ((), (), s32[]{:S(2)}) async-start(), calls=%async_computation.1 | async-start | bytes 131072 | tf_op jit(solution)/shard_map/psum | solution.py:197
  13.9 31.7 %collective-permute-start.7 = (f32[64,16]{0,1:T(8,128)S(1)}, f32[64,16]{0,1:T(8,128)S(1)}, u32[]{:S(2)}, u32[]{:S(2)}) collective-permute-start(f32[64,16]{0,1:T(8,128)S(1)} %fusion.125), channel_id=1, source_target_pairs={{16,0},{18,2},{20,4},{22,6},{24,8},{26,10},{28,12},{30,14},{32,16}... | collective-permute-start | bytes 12296 | tf_op jit(solution)/shard_map/ppermute | solution.py:19
  15.2 31.7 %collective-permute-start.6 = (f32[64,16]{0,1:T(8,128)S(1)}, f32[64,16]{0,1:T(8,128)S(1)}, u32[]{:S(2)}, u32[]{:S(2)}) collective-permute-start(f32[64,16]{0,1:T(8,128)S(1)} %fusion.125), channel_id=1, source_target_pairs={{14,0},{16,2},{18,4},{20,6},{22,8},{24,10},{26,12},{28,14},{30,16}... | collective-permute-start | bytes 12296 | tf_op jit(solution)/shard_map/ppermute | solution.py:19
  16.5 31.7 %collective-permute-start.5 = (f32[64,16]{0,1:T(8,128)S(1)}, f32[64,16]{0,1:T(8,128)S(1)}, u32[]{:S(2)}, u32[]{:S(2)}) collective-permute-start(f32[64,16]{0,1:T(8,128)S(1)} %fusion.125), channel_id=1, source_target_pairs={{12,0},{14,2},{16,4},{18,6},{20,8},{22,10},{24,12},{26,14},{28,16}... | collective-permute-start | bytes 12296 | tf_op jit(solution)/shard_map/ppermute | solution.py:19
  17.8 40.2 %collective-permute-start.4 = (f32[64,16]{0,1:T(8,128)S(1)}, f32[64,16]{0,1:T(8,128)S(1)}, u32[]{:S(2)}, u32[]{:S(2)}) collective-permute-start(f32[64,16]{0,1:T(8,128)S(1)} %fusion.125), channel_id=1, source_target_pairs={{10,0},{12,2},{14,4},{16,6},{18,8},{20,10},{22,12},{24,14},{26,16}... | collective-permute-start | bytes 12296 | tf_op jit(solution)/shard_map/ppermute | solution.py:19
  19.1 43.1 %collective-permute-start.3 = (f32[64,16]{0,1:T(8,128)S(1)}, f32[64,16]{0,1:T(8,128)S(1)}, u32[]{:S(2)}, u32[]{:S(2)}) collective-permute-start(f32[64,16]{0,1:T(8,128)S(1)} %fusion.125), channel_id=1, source_target_pairs={{8,0},{10,2},{12,4},{14,6},{16,8},{18,10},{20,12},{22,14},{24,16},... | collective-permute-start | bytes 12296 | tf_op jit(solution)/shard_map/ppermute | solution.py:19
  31.7 32.5 %copy-start.15 = (bf16[16,1,3,16]{3,0,2,1:T(8,128)(2,1)}, bf16[16,1,3,16]{3,0,2,1:T(8,128)(2,1)S(1)}, u32[]{:S(2)}) copy-start(bf16[16,1,3,16]{3,0,2,1:T(8,128)(2,1)S(1)} %get-tuple-element.88) | copy-start | bytes 4612
  31.7 32.5 %copy-start.17 = (bf16[16,1,3,16]{3,0,2,1:T(8,128)(2,1)}, bf16[16,1,3,16]{3,0,2,1:T(8,128)(2,1)S(1)}, u32[]{:S(2)}) copy-start(bf16[16,1,3,16]{3,0,2,1:T(8,128)(2,1)S(1)} %get-tuple-element.89) | copy-start | bytes 4612
  32.7 41.3 %copy-start.9 = (f32[16,64]{0,1:T(8,128)}, f32[16,64]{0,1:T(8,128)S(1)}, u32[]{:S(2)}) copy-start(f32[16,64]{0,1:T(8,128)S(1)} %fusion.124) | copy-start | bytes 12292
  35.0 39.0 %copy-start.6 = (f32[64,512]{1,0:T(8,128)}, f32[64,512]{1,0:T(8,128)S(1)}, u32[]{:S(2)}) copy-start(f32[64,512]{1,0:T(8,128)S(1)} %and_convert_fusion) | copy-start | bytes 393220
  45.6 18.5 %collective-permute-start.2 = (f32[64,16]{0,1:T(8,128)S(1)}, f32[64,16]{0,1:T(8,128)S(1)}, u32[]{:S(2)}, u32[]{:S(2)}) collective-permute-start(f32[64,16]{0,1:T(8,128)S(1)} %fusion.125), channel_id=1, source_target_pairs={{6,0},{8,2},{10,4},{12,6},{14,8},{16,10},{18,12},{20,14},{22,16},{... | collective-permute-start | bytes 12296 | tf_op jit(solution)/shard_map/ppermute | solution.py:19
  46.9 17.3 %collective-permute-start.1 = (f32[64,16]{0,1:T(8,128)S(1)}, f32[64,16]{0,1:T(8,128)S(1)}, u32[]{:S(2)}, u32[]{:S(2)}) collective-permute-start(f32[64,16]{0,1:T(8,128)S(1)} %fusion.125), channel_id=1, source_target_pairs={{4,0},{6,2},{8,4},{10,6},{12,8},{14,10},{16,12},{18,14},{20,16},{2... | collective-permute-start | bytes 12296 | tf_op jit(solution)/shard_map/ppermute | solution.py:19
  48.2 16.0 %collective-permute-start = (f32[64,16]{0,1:T(8,128)S(1)}, f32[64,16]{0,1:T(8,128)S(1)}, u32[]{:S(2)}, u32[]{:S(2)}) collective-permute-start(f32[64,16]{0,1:T(8,128)S(1)} %fusion.125), channel_id=1, source_target_pairs={{2,0},{4,2},{6,4},{8,6},{10,8},{12,10},{14,12},{16,14},{18,16},{20... | collective-permute-start | bytes 12296 | tf_op jit(solution)/shard_map/ppermute | solution.py:19
  58.0 23.5 %collective-permute-start.12 = (bf16[8,512]{1,0:T(8,128)(2,1)}, bf16[8,512]{1,0:T(8,128)(2,1)}, u32[]{:S(2)}, u32[]{:S(2)}) collective-permute-start(bf16[8,512]{1,0:T(8,128)(2,1)} %get-tuple-element.74), channel_id=1, source_target_pairs={{0,2},{2,4},{4,6},{6,8},{8,10},{10,12},{12,14},{14,16},{16,18},{18... | collective-permute-start | bytes 24584 | tf_op jit(solution)/shard_map/ppermute | solution.py:27
  62.2 19.3 %collective-permute-start.13 = (bf16[8,512]{1,0:T(8,128)(2,1)}, bf16[8,512]{1,0:T(8,128)(2,1)}, u32[]{:S(2)}, u32[]{:S(2)}) collective-permute-start(bf16[8,512]{1,0:T(8,128)(2,1)} %get-tuple-element.75), channel_id=1, source_target_pairs={{2,0},{4,2},{6,4},{8,6},{10,8},{12,10},{14,12},{16,14},{18,16},{20... | collective-permute-start | bytes 24584 | tf_op jit(solution)/shard_map/ppermute | solution.py:30
  75.4 16.2 %collective-permute-start.8 = (bf16[16,8,512]{2,0,1:T(8,128)(2,1)S(1)}, bf16[16,8,512]{2,0,1:T(8,128)(2,1)S(1)}, u32[]{:S(2)}, u32[]{:S(2)}) collective-permute-start(bf16[16,8,512]{2,0,1:T(8,128)(2,1)S(1)} %get-tuple-element.72), channel_id=1, source_target_pairs={{0,2},{2,4},{4,6},{6,8},{8,10},{10,12},{12,14},{14,16},{16,18},{18... | collective-permute-start | bytes 393224 | tf_op jit(solution)/shard_map/ppermute | solution.py:27
  79.0 12.5 %collective-permute-start.9 = (bf16[16,8,512]{2,0,1:T(8,128)(2,1)S(1)}, bf16[16,8,512]{2,0,1:T(8,128)(2,1)S(1)}, u32[]{:S(2)}, u32[]{:S(2)}) collective-permute-start(bf16[16,8,512]{2,0,1:T(8,128)(2,1)S(1)} %get-tuple-element.73), channel_id=1, source_target_pairs={{2,0},{4,2},{6,4},{8,6},{10,8},{12,10},{14,12},{16,14},{18,16},{20... | collective-permute-start | bytes 393224 | tf_op jit(solution)/shard_map/ppermute | solution.py:30
  110.8 16.8 %collective-permute-start.10 = (bf16[16,8,512]{2,0,1:T(8,128)(2,1)}, bf16[16,8,512]{2,0,1:T(8,128)(2,1)}, u32[]{:S(2)}, u32[]{:S(2)}) collective-permute-start(bf16[16,8,512]{2,0,1:T(8,128)(2,1)} %get-tuple-element.70), channel_id=1, source_target_pairs={{0,2},{2,4},{4,6},{6,8},{8,10},{10,12},{12,14},{14,16},{16,18},{18... | collective-permute-start | bytes 393224 | tf_op jit(solution)/shard_map/ppermute | solution.py:27
  114.4 13.3 %collective-permute-start.11 = (bf16[16,8,512]{2,0,1:T(8,128)(2,1)}, bf16[16,8,512]{2,0,1:T(8,128)(2,1)}, u32[]{:S(2)}, u32[]{:S(2)}) collective-permute-start(bf16[16,8,512]{2,0,1:T(8,128)(2,1)} %get-tuple-element.71), channel_id=1, source_target_pairs={{2,0},{4,2},{6,4},{8,6},{10,8},{12,10},{14,12},{16,14},{18,16},{20... | collective-permute-start | bytes 393224 | tf_op jit(solution)/shard_map/ppermute | solution.py:30
  120.6 22.9 %collective-permute-start.14 = (bf16[16,8,512]{2,0,1:T(8,128)(2,1)}, bf16[16,8,512]{2,0,1:T(8,128)(2,1)S(1)}, u32[]{:S(2)}, u32[]{:S(2)}) collective-permute-start(bf16[16,8,512]{2,0,1:T(8,128)(2,1)} %get-tuple-element.68), channel_id=1, source_target_pairs={{0,2},{2,4},{4,6},{6,8},{8,10},{10,12},{12,14},{14,16},{16,18},{18... | collective-permute-start | bytes 393224 | tf_op jit(solution)/shard_map/ppermute | solution.py:27
  124.3 19.3 %collective-permute-start.15 = (bf16[16,8,512]{2,0,1:T(8,128)(2,1)}, bf16[16,8,512]{2,0,1:T(8,128)(2,1)S(1)}, u32[]{:S(2)}, u32[]{:S(2)}) collective-permute-start(bf16[16,8,512]{2,0,1:T(8,128)(2,1)} %get-tuple-element.69), channel_id=1, source_target_pairs={{2,0},{4,2},{6,4},{8,6},{10,8},{12,10},{14,12},{16,14},{18,16},{20... | collective-permute-start | bytes 393224 | tf_op jit(solution)/shard_map/ppermute | solution.py:30
  164.0 56.0 %copy-start.12 = (bf16[512,16]{0,1:T(8,128)(2,1)S(1)}, bf16[512,16]{0,1:T(8,128)(2,1)}, u32[]{:S(2)}) copy-start(bf16[512,16]{0,1:T(8,128)(2,1)} %param.11) | copy-start | bytes 49156
  164.3 37.7 %collective-permute-start.16 = (f32[16,64]{1,0:T(8,128)S(1)}, f32[16,64]{1,0:T(8,128)S(1)}, u32[]{:S(2)}, u32[]{:S(2)}) collective-permute-start(f32[16,64]{1,0:T(8,128)S(1)} %get-tuple-element.76), channel_id=1, source_target_pairs={{0,2},{2,4},{4,6},{6,8},{8,10},{10,12},{12,14},{14,16},{16,18},{18... | collective-permute-start | bytes 12296 | tf_op jit(solution)/shard_map/ppermute | solution.py:19
  168.0 45.1 %collective-permute-start.23 = (f32[16,64]{1,0:T(8,128)S(1)}, f32[16,64]{1,0:T(8,128)S(1)}, u32[]{:S(2)}, u32[]{:S(2)}) collective-permute-start(f32[16,64]{1,0:T(8,128)S(1)} %get-tuple-element.77), channel_id=1, source_target_pairs={{0,16},{2,18},{4,20},{6,22},{8,24},{10,26},{12,28},{14,30},{16,32}... | collective-permute-start | bytes 12296 | tf_op jit(solution)/shard_map/ppermute | solution.py:19
  180.1 34.3 %collective-permute-start.22 = (f32[16,64]{1,0:T(8,128)S(1)}, f32[16,64]{1,0:T(8,128)S(1)}, u32[]{:S(2)}, u32[]{:S(2)}) collective-permute-start(f32[16,64]{1,0:T(8,128)S(1)} %get-tuple-element.78), channel_id=1, source_target_pairs={{0,14},{2,16},{4,18},{6,20},{8,22},{10,24},{12,26},{14,28},{16,30}... | collective-permute-start | bytes 12296 | tf_op jit(solution)/shard_map/ppermute | solution.py:19
  196.6 1006.6 %all-reduce.12.cloned.1.call-start = ((), (), s32[]{:S(2)}) async-start(), calls=%async_computation.3 | async-start | bytes 525312 | tf_op jit(solution)/shard_map/psum | solution.py:246
  196.7 22.4 %collective-permute-start.21 = (f32[16,64]{1,0:T(8,128)S(1)}, f32[16,64]{1,0:T(8,128)S(1)}, u32[]{:S(2)}, u32[]{:S(2)}) collective-permute-start(f32[16,64]{1,0:T(8,128)S(1)} %get-tuple-element.79), channel_id=1, source_target_pairs={{0,12},{2,14},{4,16},{6,18},{8,20},{10,22},{12,24},{14,26},{16,28}... | collective-permute-start | bytes 12296 | tf_op jit(solution)/shard_map/ppermute | solution.py:19
  200.7 18.4 %collective-permute-start.20 = (f32[16,64]{1,0:T(8,128)S(1)}, f32[16,64]{1,0:T(8,128)S(1)}, u32[]{:S(2)}, u32[]{:S(2)}) collective-permute-start(f32[16,64]{1,0:T(8,128)S(1)} %get-tuple-element.80), channel_id=1, source_target_pairs={{0,10},{2,12},{4,14},{6,16},{8,18},{10,20},{12,22},{14,24},{16,26}... | collective-permute-start | bytes 12296 | tf_op jit(solution)/shard_map/ppermute | solution.py:19
  202.0 17.1 %collective-permute-start.19 = (f32[16,64]{1,0:T(8,128)S(1)}, f32[16,64]{1,0:T(8,128)S(1)}, u32[]{:S(2)}, u32[]{:S(2)}) collective-permute-start(f32[16,64]{1,0:T(8,128)S(1)} %get-tuple-element.81), channel_id=1, source_target_pairs={{0,8},{2,10},{4,12},{6,14},{8,16},{10,18},{12,20},{14,22},{16,24},... | collective-permute-start | bytes 12296 | tf_op jit(solution)/shard_map/ppermute | solution.py:19
  213.1 6.0 collective-permute-start.18
  214.4 4.8 collective-permute-start.17
  219.9 1001.9 %reduce-scatter.2.cloned.1.call-start = ((), (), s32[]{:S(2)}) async-start(), calls=%async_computation.2 | async-start | bytes 98304 | tf_op jit(solution)/shard_map/reduce_scatter | solution.py:236
  (37 other events, 380.9 us)
Sparse Core Ops, SparseCore 0:
  196.7 41.9 all-reduce.9
  242.3 960.8 all-reduce.11
  1206.3 15.4 reduce-scatter.1
where the time goes:
time: 1240 us; the launch traced here: 1230 us
  waiting for transfers between devices  995 us (80%)
  starting transfers between devices  90.2 us (7%)
  local copies, waits for them, and re-layouts  58 us (5%)
  matrix products  29.8 us (2%)
  between operations  29.3 us (2%)
  other arithmetic  20.5 us (2%)
    psum x1, waiting for transfers between devices, on_device(): lax.psum((left_wpart, right_wpart, first_weight_gradient, second_weight_g...  963 us
    ppermute x16, starting transfers between devices, from_behind(): return lax.ppermute(block, axis, route)  66.9 us
  transfers between devices with their start and end apart: 27, of which 4 were waited for; matrix products, arithmetic and copies ran while one was open for 6% of the time, Pallas kernels for 0%

commit v1 on v0

v1 whole, which is shorter than its diff:
```python
import functools
import math

import jax
import jax.numpy as jnp
from jax import lax
from jax.experimental import pallas as pl
from jax.experimental.pallas import tpu as pltpu
from jax.sharding import PartitionSpec as P

MESH = pl.DeviceIdType.MESH
ROWS = 64
BEHIND = 9

OFF = 512
LANES = 128
TILES = OFF // LANES
TAPS = (-1, 0, 1)
INV_ROOT_TWO = 0.7071067811865476
INV_ROOT_TWO_PI = 0.3989422804014327


def lane_ids(rows):
    return lax.broadcasted_iota(jnp.int32, (rows, LANES), 1)


def shift_tiles(tiles, count, dist):
    if count == 0:
        return tiles
    lane = lane_ids(tiles[0].shape[0])
    zero = jnp.zeros_like(tiles[0])
    if count > 0:
        amount = count * dist
        rolled = [pltpu.roll(t, amount, 1) for t in tiles]
        before = [zero] + rolled[:-1]
        return [jnp.where(lane < amount, b, r) for b, r in zip(before, rolled)]
    amount = LANES + count * dist
    rolled = [pltpu.roll(t, amount, 1) for t in tiles]
    after = rolled[1:] + [zero]
    return [jnp.where(lane < amount, r, a) for r, a in zip(rolled, after)]


def local_kernel(
    ends, dil, rb, lb, cot, w1, w1t, vm, zw, head,
    contact, lg, rg, gconv, acc,
    px, gy, band, vga, z, reach,
    *, unroll,
):
    row0 = lax.axis_index("chrom") * 64 - 16
    d1 = dil[0]
    d2 = dil[1]
    big = jnp.int32(1 << 30)

    ids = lax.broadcasted_iota(jnp.int32, (96, LANES), 0) + row0
    nxt = jnp.full((96, LANES), big)
    for j in range(8):
        nxt = jnp.minimum(nxt, jnp.where(ends[j] > ids, ends[j], big))
    width = jnp.where((ids >= 0) & (nxt < big), nxt - ids, 0)
    lane96 = lane_ids(96)
    vg = [
        jnp.where(
            lane96 + t * LANES < width, cot[:, t * LANES : (t + 1) * LANES].astype(jnp.float32), 0.0
        )
        for t in range(TILES)
    ]
    for e in range(-2, 3):
        for t, tile in enumerate(shift_tiles(vg, e, d2)):
            vga[t, pl.ds(e + 2, 96, stride=8), :] = tile
    for e in range(5, 8):
        for t in range(TILES):
            vga[t, pl.ds(e, 96, stride=8), :] = jnp.zeros((96, LANES), jnp.float32)

    lane = lane_ids(16)

    def pair_row(q):
        i = row0 + q
        m = big
        for j in range(8):
            m = jnp.minimum(m, jnp.where(ends[j] > i, ends[j], big))
        n = jnp.where((i >= 0) & (m < big), m - i, 0)
        reach[q] = n
        back = lax.rem(LANES - q, LANES)
        rolled = [pltpu.roll(rb[:, t * LANES : (t + 1) * LANES], back, 1) for t in range(TILES + 1)]
        left = pltpu.roll(lb[...], back, 1)[:, 0:1]
        tiles = []
        for t in range(TILES):
            b = jnp.where(lane < LANES - q, rolled[t], rolled[t + 1])
            band[q, :, t * LANES : (t + 1) * LANES] = b
            tiles.append(jnp.where(lane + t * LANES < n, left * b, 0.0).astype(jnp.bfloat16))
        for e in range(-2, 3):
            for t, tile in enumerate(shift_tiles(tiles, -e, d1)):
                px[e + 2, q, :, t * LANES : (t + 1) * LANES] = tile

    def loop(start, count, body, init=None):
        if init is None:
            def step(s, _):
                for u in range(unroll):
                    body(start + s * unroll + u)
                return 0
            lax.fori_loop(0, count // unroll, step, 0)
            return None

        def step(s, carry):
            for u in range(unroll):
                carry = body(start + s * unroll + u, carry)
            return carry
        return lax.fori_loop(0, count // unroll, step, init)

    loop(0, 96, pair_row)

    lane512 = lax.broadcasted_iota(jnp.int32, (16, OFF), 1)

    def hidden_row(q, carry):
        g_acc, a_acc = carry
        stack = jnp.concatenate(
            [px[b - a + 2, q + a * d1] for a in TAPS for b in TAPS], axis=0
        )
        mask = lane512 < reach[q]
        first = jnp.where(mask, jnp.dot(w1[...], stack, preferred_element_type=jnp.float32), 0.0)
        cdf = 0.5 * (1.0 + lax.erf(first * INV_ROOT_TWO))
        slope = cdf + first * jnp.exp(-0.5 * first * first) * INV_ROOT_TWO_PI
        hidden = (first * cdf).astype(jnp.bfloat16)
        vstack = jnp.concatenate(
            [
                jnp.concatenate(
                    [vga[t, pl.ds(pl.multiple_of((q - a * d2) * 8, 8), 8), :] for a in TAPS], axis=0
                )
                for t in range(TILES)
            ],
            axis=1,
        ).astype(jnp.bfloat16)
        both = jnp.dot(vm[...], vstack, preferred_element_type=jnp.float32)
        grad_hidden = both[:16] + both[16:]
        gf = jnp.where(mask, slope * grad_hidden, 0.0).astype(jnp.bfloat16)
        tiles = [gf[:, t * LANES : (t + 1) * LANES] for t in range(TILES)]
        for e in range(-2, 3):
            for t, tile in enumerate(shift_tiles(tiles, e, d1)):
                gy[e + 2, q, :, t * LANES : (t + 1) * LANES] = tile
        hp = jnp.concatenate([hidden, px[2, q]], axis=0)
        zz = jnp.dot(zw[...], hp, preferred_element_type=jnp.float32)
        zz = zz[:16] + zz[16:]
        for t in range(TILES):
            z[t, pl.ds(pl.multiple_of(q * 16, 16), 16), :] = zz[:, t * LANES : (t + 1) * LANES]
        own = jnp.where((q >= 16) & (q < 80), 1.0, 0.0).astype(jnp.float32)
        last = (((1,), (1,)), ((), ()))
        g_acc = g_acc + own * lax.dot_general(gf, stack, last, preferred_element_type=jnp.float32)
        a_acc = a_acc + own * lax.dot_general(vstack, hp, last, preferred_element_type=jnp.float32)
        return g_acc, a_acc

    g_acc, a_acc = loop(
        8, 80, hidden_row, (jnp.zeros((16, 144), jnp.float32), jnp.zeros((24, 32), jnp.float32))
    )
    gconv[...] = jnp.zeros((16, 256), jnp.float32)
    gconv[:, :144] = g_acc
    acc[...] = jnp.zeros((24, LANES), jnp.float32)
    acc[:, :32] = a_acc

    lg[...] = jnp.zeros((16, LANES), jnp.float32)
    rg[...] = jnp.zeros((16, 5 * LANES), jnp.float32)

    def grad_row(q, carry):
        lg_acc, rg_acc = carry
        rr = q - 16
        stack = jnp.concatenate(
            [gy[b - a + 2, q - a * d1] for a in TAPS for b in TAPS], axis=0
        )
        grad_pair = jnp.dot(w1t[...], stack, preferred_element_type=jnp.float32)
        n = reach[q]
        left = pltpu.roll(lb[...], lax.rem(LANES - q, LANES), 1)[:, 0:1]
        prods = []
        spread = []
        for t in range(TILES):
            cols = slice(t * LANES, (t + 1) * LANES)
            g = vga[t, pl.ds(q * 8 + 2, 1), :]
            gp = jnp.where(lane + t * LANES < n, grad_pair[:, cols] + head[...] * g, 0.0)
            prods.append(gp * band[q, :, cols])
            spread.append(pltpu.roll(gp * left, rr, 1))
        total = (prods[0] + prods[1]) + (prods[2] + prods[3])
        lg_acc = jnp.where(lane == rr, jnp.sum(total, axis=1, keepdims=True), lg_acc)
        zero = jnp.zeros((16, LANES), jnp.float32)
        before = [zero] + spread
        after = spread + [zero]
        rg_acc = tuple(
            r + jnp.where(lane < rr, b, a) for r, b, a in zip(rg_acc, before, after)
        )
        return lg_acc, rg_acc

    zero = jnp.zeros((16, LANES), jnp.float32)
    lg_acc, rg_acc = loop(16, 64, grad_row, (zero, (zero,) * (TILES + 1)))
    lg[...] = lg_acc
    for t in range(TILES + 1):
        rg[:, t * LANES : (t + 1) * LANES] = rg_acc[t]

    def zrows(t, a, row):
        return z[t, pl.ds((16 + a * d2) * 16 + row, 64, stride=16), :]

    total = None
    for e in range(-2, 3):
        parts = [
            sum(zrows(t, a, (a + 1) * 3 + a + e + 1) for a in TAPS if -1 <= a + e <= 1)
            for t in range(TILES)
        ]
        parts = shift_tiles(parts, -e, d2)
        total = parts if total is None else [x + y for x, y in zip(total, parts)]
    lane64 = lane_ids(64)
    for t in range(TILES):
        contact[:, t * LANES : (t + 1) * LANES] = zrows(t, 0, 9) + jnp.where(
            lane64 + t * LANES < width[16:80], total[t], 0.0
        )


def weight_forms(first_w, second_w, head):
    w1 = first_w.reshape(16, 144)
    w1t = jnp.transpose(first_w, (3, 1, 2, 0)).reshape(16, 144)
    v = jnp.sum(second_w.astype(jnp.float32) * head[:, None, None, None], axis=0)
    def split(m):
        hi = m.astype(jnp.bfloat16)
        lo = (m - hi.astype(jnp.float32)).astype(jnp.bfloat16)
        return jnp.concatenate([hi, lo], axis=0)
    vt = jnp.transpose(v, (2, 0, 1))
    vm = jnp.concatenate(
        [jnp.pad(vt[:, a], ((0, 0), (2 - a, 3 + a))) for a in range(3)], axis=1
    )
    zw = jnp.concatenate(
        [
            jnp.pad(v.reshape(9, 16), ((0, 0), (0, 16))),
            jnp.pad(head[None], ((0, 0), (16, 0))),
            jnp.zeros((6, 32), jnp.float32),
        ],
        axis=0,
    )
    return w1, w1t, split(vm), split(zw)


def local_call(ends, dil, rb, lb, cot96, w1, w1t, vm, zw, head_col, unroll=2):
    v = pl.BlockSpec(memory_space=pltpu.VMEM)
    s = pl.BlockSpec(memory_space=pltpu.SMEM)
    f32 = jnp.float32
    return pl.pallas_call(
        functools.partial(local_kernel, unroll=unroll),
        out_shape=(
            jax.ShapeDtypeStruct((64, OFF), f32),
            jax.ShapeDtypeStruct((16, LANES), f32),
            jax.ShapeDtypeStruct((16, 5 * LANES), f32),
            jax.ShapeDtypeStruct((16, 256), f32),
            jax.ShapeDtypeStruct((24, LANES), f32),
        ),
        in_specs=[s, s] + [v] * 8,
        out_specs=[v] * 5,
        scratch_shapes=[
            pltpu.VMEM((5, 96, 16, OFF), jnp.bfloat16),
            pltpu.VMEM((5, 96, 16, OFF), jnp.bfloat16),
            pltpu.VMEM((96, 16, OFF), f32),
            pltpu.VMEM((TILES, 96 * 8, LANES), f32),
            pltpu.VMEM((TILES, 96 * 16, LANES), f32),
            pltpu.SMEM((96,), jnp.int32),
        ],
        compiler_params=pltpu.CompilerParams(vmem_limit_bytes=52 * 1024 * 1024),
    )(ends, dil, rb, lb, cot96, w1, w1t, vm, zw, head_col)


def peer(chrom, chan):
    return {"chrom": chrom, "chan": chan}


def hop(me, distance):
    count = lax.axis_size("chrom")
    return lax.rem(me + distance + count, count)


def gather_kernel(
    emb, wt, cot, full, rb, lb, cot96, wother, slots, send_sem, recv_sem,
):
    me = lax.axis_index("chrom")
    half = lax.axis_index("chan")
    other = 1 - half
    barrier = pltpu.get_barrier_semaphore()
    sources = [(hop(me, d), half) for d in range(1, BEHIND + 1)]
    sources += [(hop(me, -1), half), (me, other)]
    for chrom, chan in sources:
        pl.semaphore_signal(barrier, inc=1, device_id=peer(chrom, chan), device_id_type=MESH)
    pl.semaphore_wait(barrier, len(sources))

    def copy(index, src, dst, chrom, chan):
        c = pltpu.make_async_remote_copy(
            src_ref=src, dst_ref=dst, send_sem=send_sem.at[index], recv_sem=recv_sem.at[index],
            device_id=peer(chrom, chan), device_id_type=MESH,
        )
        c.start()
        return c

    mine = pl.ds(pl.multiple_of(half * 256, 256), 256)
    theirs = pl.ds(pl.multiple_of(other * 256, 256), 256)
    first = copy(0, emb, full.at[:, mine], me, other)
    rest = [
        copy(1, wt.at[:, theirs], wother, me, other),
        copy(2, cot.at[pl.ds(48, 16)], cot96.at[pl.ds(0, 16)], hop(me, 1), half),
        copy(3, cot.at[pl.ds(0, 16)], cot96.at[pl.ds(80, 16)], hop(me, -1), half),
    ]
    full[:, mine] = emb[...]
    cot96[16:80, :] = cot[...]
    first.wait_recv()
    twice = jnp.concatenate([full[...], full[...]], axis=0)
    last = (((1,), (1,)), ((), ()))
    left2 = lax.dot_general(wt[0:16, :], twice, last, preferred_element_type=jnp.float32)
    right2 = lax.dot_general(wt[16:32, :], twice, last, preferred_element_type=jnp.float32)
    lane = lane_ids(16)
    slots[1] = jnp.where(lane < ROWS, right2, left2)
    for d in range(1, BEHIND + 1):
        rest.append(copy(3 + d, slots.at[1], slots.at[1 + d], hop(me, -d), half))
    rest.append(copy(4 + BEHIND, slots.at[1], slots.at[0], hop(me, 1), half))
    first.wait_send()
    for c in rest:
        c.wait()
    for t in range(TILES + 1):
        low = pltpu.roll(slots[2 * t], 80, 1)
        mid = pltpu.roll(slots[2 * t + 1], 16, 1)
        high = pltpu.roll(slots[2 * t + 2], 80, 1)
        rb[:, t * LANES : (t + 1) * LANES] = jnp.where(
            lane < 16, low, jnp.where(lane < 80, mid, high)
        )
    lb[...] = jnp.where(
        lane < 16,
        pltpu.roll(slots[0], 16, 1),
        jnp.where(lane < 80, pltpu.roll(slots[1], 80, 1), pltpu.roll(slots[2], 16, 1)),
    )


def gather_call(emb, wt, cot):
    v = pl.BlockSpec(memory_space=pltpu.VMEM)
    f32, bf16 = jnp.float32, jnp.bfloat16
    copies = 5 + BEHIND
    return pl.pallas_call(
        gather_kernel,
        out_shape=(
            jax.ShapeDtypeStruct((ROWS, 512), bf16),
            jax.ShapeDtypeStruct((16, 5 * LANES), f32),
            jax.ShapeDtypeStruct((16, LANES), f32),
            jax.ShapeDtypeStruct((96, OFF), bf16),
            jax.ShapeDtypeStruct((32, 256), bf16),
        ),
        in_specs=[v] * 3,
        out_specs=[v] * 5,
        scratch_shapes=[
            pltpu.VMEM((BEHIND + 2, 16, LANES), f32),
            pltpu.SemaphoreType.DMA((copies,)),
            pltpu.SemaphoreType.DMA((copies,)),
        ],
        compiler_params=pltpu.CompilerParams(
            collective_id=0, has_side_effects=True, vmem_limit_bytes=16 * 1024 * 1024
        ),
    )(emb, wt, cot)


def reduce_kernel(
    scale, contact, rg, lg, gconv, acc, full, wt, wother,
    contacts, emb_grad, fin,
    csend, crecv, rsend, rrecv, lrsend, lrrecv, buf, arecv, brecv, send_sem, recv_sem,
):
    me = lax.axis_index("chrom")
    half = lax.axis_index("chan")
    other = 1 - half
    place = lax.rem(me, 16)
    plane = me // 16
    base = me - place
    group = [base + lax.rem(place + s, 16) for s in range(1, 16)]
    column = [lax.rem(plane + s, 8) for s in range(1, 8)]

    barrier = pltpu.get_barrier_semaphore()
    sources = [(hop(me, -d), half) for d in range(1, 9)] + [(me, other)]
    sources += [(g, half) for g in group] + [(p * 16 + place, half) for p in column]
    for chrom, chan in sources:
        pl.semaphore_signal(barrier, inc=1, device_id=peer(chrom, chan), device_id_type=MESH)

    csend[...] = contact[...].astype(jnp.bfloat16)
    for d in range(1, 9):
        piece = rg[:, (d // 2) * LANES : (d // 2 + 1) * LANES]
        rsend[d] = pltpu.roll(piece, 64, 1) if d % 2 else piece
    pl.semaphore_wait(barrier, len(sources))

    def copy(send, recv, src, dst, chrom, chan):
        c = pltpu.make_async_remote_copy(
            src_ref=src, dst_ref=dst, send_sem=send_sem.at[send], recv_sem=recv_sem.at[recv],
            device_id=peer(chrom, chan), device_id_type=MESH,
        )
        c.start()
        return c

    rights = [
        copy(d, d, rsend.at[d], rrecv.at[d], hop(me, d), half) for d in range(1, 9)
    ]
    swap = copy(0, 0, csend, crecv, me, other)
    lane = lane_ids(16)
    for c in rights:
        c.wait()
    right = rg[:, :LANES]
    for d in range(1, 9):
        right = right + rrecv[d]
    right = jnp.where(lane < ROWS, right, 0.0)
    lrsend[...] = jnp.concatenate([lg[...], right], axis=0).astype(jnp.bfloat16)
    trade = copy(9, 9, lrsend, lrrecv, me, other)

    wpart = jnp.dot(lrsend[:, :ROWS], full[...], preferred_element_type=jnp.float32)
    for j in range(16):
        i, t = j // 4, j % 4
        buf[j, 0:8, :] = wpart[8 * i : 8 * i + 8, t * LANES : (t + 1) * LANES]
        if j < 4:
            buf[j, 8:16, :] = gconv[8 * (j // 2) : 8 * (j // 2) + 8, (j % 2) * LANES : (j % 2 + 1) * LANES]
        elif j < 7:
            buf[j, 8:16, :] = acc[8 * (j - 4) : 8 * (j - 3), :]
        else:
            buf[j, 8:16, :] = jnp.zeros((8, LANES), jnp.float32)
    stage = []
    for s in range(1, 16):
        target = lax.rem(place + s, 16)
        stage.append(copy(9 + s, 9 + s, buf.at[target], arecv.at[s], base + target, half))

    swap.wait()
    contacts[...] = csend[...].astype(jnp.float32) + crecv[...].astype(jnp.float32)
    trade.wait()
    both = jnp.concatenate([lrsend[...], lrrecv[...]], axis=0)
    mine = pl.ds(pl.multiple_of(half * 256, 256), 256)
    weights = jnp.concatenate([wt[:, mine], wother[...]], axis=0)
    grads = lax.dot_general(
        both, weights, (((0,), (0,)), ((), ())), preferred_element_type=jnp.float32
    )
    emb_grad[...] = grads[:ROWS].astype(jnp.bfloat16)

    total = buf[place]
    for s, c in enumerate(stage):
        c.wait()
        total = total + arecv[s + 1]
    brecv[plane] = total
    stage = []
    for s in range(1, 8):
        target = lax.rem(plane + s, 8)
        stage.append((s, pltpu.make_async_remote_copy(
            src_ref=brecv.at[plane], dst_ref=brecv.at[plane],
            send_sem=send_sem.at[24 + s], recv_sem=recv_sem.at[25 + plane],
            device_id=peer(target * 16 + place, half), device_id_type=MESH,
        )))
        stage[-1][1].start()
    for s, c in stage:
        c.wait_send()
        source = lax.rem(plane + s, 8)
        pltpu.make_async_remote_copy(
            src_ref=brecv.at[source], dst_ref=brecv.at[source],
            send_sem=send_sem.at[24 + s], recv_sem=recv_sem.at[25 + source],
            device_id=peer(source * 16 + place, half), device_id_type=MESH,
        ).wait_recv()
    total = brecv[0]
    for p in range(1, 8):
        total = total + brecv[p]
    fin[place] = total * scale
    stage = []
    for s in range(1, 16):
        target = lax.rem(place + s, 16)
        stage.append((s, pltpu.make_async_remote_copy(
            src_ref=fin.at[place], dst_ref=fin.at[place],
            send_sem=send_sem.at[32 + s], recv_sem=recv_sem.at[33 + place],
            device_id=peer(base + target, half), device_id_type=MESH,
        )))
        stage[-1][1].start()
    for s, c in stage:
        c.wait_send()
        source = lax.rem(place + s, 16)
        pltpu.make_async_remote_copy(
            src_ref=fin.at[source], dst_ref=fin.at[source],
            send_sem=send_sem.at[32 + s], recv_sem=recv_sem.at[33 + source],
            device_id=peer(base + source, half), device_id_type=MESH,
        ).wait_recv()


def reduce_call(scale, contact, rg, lg, gconv, acc, full, wt, wother):
    v = pl.BlockSpec(memory_space=pltpu.VMEM)
    f32, bf16 = jnp.float32, jnp.bfloat16
    return pl.pallas_call(
        functools.partial(reduce_kernel, scale),
        out_shape=(
            jax.ShapeDtypeStruct((ROWS, OFF), f32),
            jax.ShapeDtypeStruct((ROWS, 256), bf16),
            jax.ShapeDtypeStruct((16, 16, LANES), f32),
        ),
        in_specs=[v] * 8,
        out_specs=[v] * 3,
        scratch_shapes=[
            pltpu.VMEM((ROWS, OFF), bf16),
            pltpu.VMEM((ROWS, OFF), bf16),
            pltpu.VMEM((9, 16, LANES), f32),
            pltpu.VMEM((9, 16, LANES), f32),
            pltpu.VMEM((32, LANES), bf16),
            pltpu.VMEM((32, LANES), bf16),
            pltpu.VMEM((16, 16, LANES), f32),
            pltpu.VMEM((16, 16, LANES), f32),
            pltpu.VMEM((8, 16, LANES), f32),
            pltpu.SemaphoreType.DMA((49,)),
            pltpu.SemaphoreType.DMA((49,)),
        ],
        compiler_params=pltpu.CompilerParams(
            collective_id=1, has_side_effects=True, vmem_limit_bytes=16 * 1024 * 1024
        ),
    )(contact, rg, lg, gconv, acc, full, wt, wother)


def on_device(
    embeddings,
    w_left,
    w_right,
    first_conv_weight,
    second_conv_weight,
    head_weight,
    cotangent,
    dilations,
    chrom_ends,
):
    bin_total = embeddings.shape[0] * lax.axis_size("chrom")
    scale = 1.0 / math.sqrt(bin_total * OFF)
    wt = jnp.concatenate([w_left.T, w_right.T], axis=0)
    full, rb, lb, cot96, wother = gather_call(embeddings, wt, cotangent)
    forms = weight_forms(first_conv_weight, second_conv_weight, head_weight)
    head_col = jnp.broadcast_to(head_weight[:, None], (16, LANES))
    contact, lg, rg, gconv, acc = local_call(
        chrom_ends, dilations, rb, lb, cot96, *forms, head_col
    )
    contacts, emb_grad, fin = reduce_call(
        scale, contact, rg, lg, gconv, acc, full, wt, wother
    )
    weights = jnp.transpose(fin[:, :8].reshape(4, 4, 8, LANES), (0, 2, 1, 3)).reshape(32, 512)
    first_grad = jnp.transpose(fin[:4, 8:].reshape(2, 2, 8, LANES), (0, 2, 1, 3)).reshape(16, 256)
    taps = fin[4:7, 8:]
    moved = jnp.stack([taps[0, 2:5, :16], taps[1, 1:4, :16], taps[2, 0:3, :16]])
    second_grad = head_weight[:, None, None, None] * moved[None]
    head_grad = taps[1, 2, 16:32] + jnp.sum(
        second_conv_weight.astype(jnp.float32) * moved[None], axis=(1, 2, 3)
    )
    return (
        contacts,
        emb_grad,
        weights[:16].T,
        weights[16:].T,
        first_grad[:, :144].reshape(16, 3, 3, 16),
        second_grad,
        head_grad,
    )


def solution(mesh):
    in_specs = (
        P("chrom", "chan"),
        P(None, "chan"),
        P(None, "chan"),
        P("chan", None, None, None),
        P("chan", None, None, None),
        P("chan"),
        P("chrom", None),
        P(),
        P(),
    )
    out_specs = (
        P("chrom", None),
        P("chrom", "chan"),
        P(None, "chan"),
        P(None, "chan"),
        P("chan", None, None, None),
        P("chan", None, None, None),
        P("chan"),
    )
    return jax.shard_map(
        on_device, mesh=mesh, in_specs=in_specs, out_specs=out_specs, check_vma=False
    )
```

time: 1240 us -> 98.1 us (0.08)
  waiting for transfers between devices: 995 us -> 0 us
  starting transfers between devices: 90.2 us -> 0 us
  Pallas kernels: 0 us -> 87.8 us
  local copies, waits for them, and re-layouts: 58 us -> 6.5 us
  matrix products: 29.8 us -> 0 us
  between operations: 29.3 us -> 0.78 us
  other arithmetic: 20.5 us -> 2.61 us
    psum x2 -> x0, waiting for transfers between devices: 981 us -> none  [the longest x1 963 us: on_device(): lax.psum((left_wpart, right_wpart, first_weight_gradient, second_weight_g...]
    ppermute x24 -> x0, starting transfers between devices: 90.1 us -> none  [the longest x16 66.9 us: from_behind(): return lax.ppermute(block, axis, route)]
    pallas_call x0 -> x3, Pallas kernels: none -> 87.8 us  [the longest x1 43.9 us: local_call(): pl.pallas_call(functools.partial(local_kernel, unroll=unroll), out_shape=...]
    dot_general x25 -> x0, matrix products: 29.8 us -> none  [the longest x6 9.58 us: convolution_transpose(): jnp.einsum('tc,tik->cik', tap_matrix, stacked, preferred_element_type=jnp...]
    dynamic_slice x4 -> x0, local copies, waits for them, and re-layouts: 21.7 us -> none  [window(): return lax.dynamic_slice(padded, starts, (padded.shape[0], row_count, OFF))]
    reduce_scatter x1 -> x0, waiting for transfers between devices: 13.9 us -> none  [on_device(): lax.psum_scatter(emb_part.astype(jnp.bfloat16), 'chan', scatter_dimension...]
  transfers between devices with their start and end apart: 27 -> 0, of which waited for: 4 -> 0; matrix products, arithmetic and copies ran while one was open for 6% -> 0% of each run, Pallas kernels for 0% -> 0%
where the time goes in v1:
time: 98.1 us; the launch traced here: 97.7 us
  Pallas kernels  87.8 us (90%)
  local copies, waits for them, and re-layouts  6.5 us (7%)
  other arithmetic  2.61 us (3%)
    pallas_call x1, Pallas kernels, local_call(): pl.pallas_call(functools.partial(local_kernel, unroll=unroll), out_shape=...  43.9 us
    pallas_call x1, Pallas kernels, reduce_call(): pl.pallas_call(functools.partial(reduce_kernel, scale), out_shape=(jax.Sh...  25.2 us
    pallas_call x1, Pallas kernels, gather_call(): pl.pallas_call(gather_kernel, out_shape=(jax.ShapeDtypeStruct((ROWS, 512)...  18.7 us
    unnamed x22, local copies, waits for them, and re-layouts  5.18 us

profile of v1, /device:TPU:1, one launch (start us, length us, event | category | flops | bytes accessed | tf_op | source)
XLA Modules:
  0.0 97.7 jit_solution(6715148092644535212)
XLA Ops:
  0.6 0.0 copy-start.8
  0.7 0.1 pad.32.clone
  0.7 0.6 copy-done.8
  1.3 0.9 fusion
  2.2 0.1 copy.23
  2.3 0.1 copy.25
  2.3 0.1 copy.24
  2.4 0.1 subtract_convert_fusion.1
  2.5 0.1 fusion.6
  2.6 0.1 subtract_convert_fusion
  2.7 0.1 fusion.5
  2.8 0.6 copy-done.5
  3.4 0.1 copy.27.w1t
  3.4 0.1 broadcast_in_dim.8.head
  3.5 0.6 copy-done.6
  4.1 0.0 copy-done.7
  4.1 0.0 copy-start.1
  4.1 0.1 reshape.41.w1
  4.2 0.7 copy-done
  4.9 18.7 %shard_map.144 = (bf16[64,512]{1,0:T(8,128)(2,1)S(1)}, f32[16,640]{1,0:T(8,128)S(1)}, f32[16,128]{1,0:T(8,128)S(1)}, bf16[96,512]{1,0:T(8,128)(2,1)S(1)}, bf16[32,256]{1,0:T(8,128)(2,1)S(1)}) custom-call(bf16[64,256]{1,0:T(8,128)(2,1)S(1)} %copy-done.1, bf16[32,512]{1,0:T(8,128)(2,1)S(1)} %pad_maximum_fusion.wt, bf16[64,512]{1,0:T(8,128)(2,1)S(1)} %copy-done), custom_call_target="tpu_custom_call" | custom-call | tf_op jit(solution)/shard_map/pallas_call | solution.py:333
  23.7 0.6 copy-done.2
  24.3 0.0 copy-done.3
  24.4 43.9 %shard_map.145 = (f32[64,512]{1,0:T(8,128)S(1)}, f32[16,128]{1,0:T(8,128)S(1)}, f32[16,640]{1,0:T(8,128)S(1)}, f32[16,256]{1,0:T(8,128)S(1)}, f32[24,128]{1,0:T(8,128)S(1)}) custom-call(s32[8]{0:T(128)S(1)} %copy-done.2, s32[2]{0:T(128)S(1)} %copy-done.3, f32[16,640]{1,0:T(8,128)S(1)} %get-tuple-element.20.rb, f32[16,128]{1,0:T(8,128)S(1)} %get-tuple-element.21.lb, ...), custom_call_target="tpu_custom_call" | custom-call | tf_op jit(solution)/shard_map/pallas_call | solution.py:239
  68.3 25.2 %shard_map.146 = (f32[64,512]{1,0:T(8,128)S(1)}, bf16[64,256]{1,0:T(8,128)(2,1)S(1)}, f32[16,16,128]{2,1,0:T(8,128)S(1)}) custom-call(f32[64,512]{1,0:T(8,128)S(1)} %get-tuple-element.23.contact, f32[16,640]{1,0:T(8,128)S(1)} %get-tuple-element.24.rg, f32[16,128]{1,0:T(8,128)S(1)} %get-tuple-element.25.lg, f32[16,256]{1,0:T(8,128)S(1)} %get-tuple-element.26.gconv, ...), custom_call_target="tpu_custom_call" | custom-call | tf_op jit(solution)/shard_map/pallas_call | solution.py:477
  93.5 0.6 slice_bitcast_fusion
  94.2 0.1 copy-done.4
  94.3 0.8 fusion.1
  95.1 0.6 bitcast_add_fusion
  95.7 0.1 reshape.47
  95.8 0.6 copy.26
  96.5 0.7 copy.30
  97.1 0.6 copy.31
  (19 shorter events, 0.1 us)
Async XLA Ops:
  0.6 0.7 copy-start.8
  2.6 0.8 copy-start.5
  3.4 0.7 copy-start.6
  3.4 0.7 copy-start.7
  4.1 0.8 copy-start
  4.1 0.8 copy-start.1
  23.7 0.7 copy-start.2
  23.7 0.7 copy-start.3
  93.5 0.8 copy-start.4

commit v2 on v1

--- a/solution.py
+++ b/solution.py
@@ -42,9 +42,9 @@
 
 def local_kernel(
     ends, dil, rb, lb, cot, w1, w1t, vm, zw, head,
-    contact, lg, rg, gconv, acc,
-    px, gy, band, vga, z, reach,
-    *, unroll,
+    contact, lg, rg, gconv, taps,
+    acc, px, gy, hid, band, vga, z, edge, lcol,
+    *, unroll, unroll3, lag=1, lag2=2,
 ):
     row0 = lax.axis_index("chrom") * 64 - 16
     d1 = dil[0]
@@ -71,27 +71,37 @@
             vga[t, pl.ds(e, 96, stride=8), :] = jnp.zeros((96, LANES), jnp.float32)
 
     lane = lane_ids(16)
+    for t in range(TILES):
+        edge[t] = jnp.minimum(width, OFF) - t * LANES
+    for q in range(96):
+        lcol[q] = jnp.broadcast_to(lb[:, q : q + 1], (16, LANES))
+
+    def masks(q):
+        return [lane < edge[t, pl.ds(q, 1), :] for t in range(TILES)]
+
+    def band_row(p):
+        back = lax.rem(LANES - p, LANES)
+        rolled = [pltpu.roll(rb[:, t * LANES : (t + 1) * LANES], back, 1) for t in range(TILES + 1)]
+        for t in range(TILES):
+            band[p, :, t * LANES : (t + 1) * LANES] = jnp.where(
+                lane < LANES - p, rolled[t], rolled[t + 1]
+            )
 
     def pair_row(q):
-        i = row0 + q
-        m = big
-        for j in range(8):
-            m = jnp.minimum(m, jnp.where(ends[j] > i, ends[j], big))
-        n = jnp.where((i >= 0) & (m < big), m - i, 0)
-        reach[q] = n
-        back = lax.rem(LANES - q, LANES)
-        rolled = [pltpu.roll(rb[:, t * LANES : (t + 1) * LANES], back, 1) for t in range(TILES + 1)]
-        left = pltpu.roll(lb[...], back, 1)[:, 0:1]
-        tiles = []
-        for t in range(TILES):
-            b = jnp.where(lane < LANES - q, rolled[t], rolled[t + 1])
-            band[q, :, t * LANES : (t + 1) * LANES] = b
-            tiles.append(jnp.where(lane + t * LANES < n, left * b, 0.0).astype(jnp.bfloat16))
+        left = lcol[q]
+        ends_at = [edge[t, pl.ds(q, 1), :] for t in range(TILES)]
         for e in range(-2, 3):
-            for t, tile in enumerate(shift_tiles(tiles, -e, d1)):
-                px[e + 2, q, :, t * LANES : (t + 1) * LANES] = tile
-
-    def loop(start, count, body, init=None):
+            move = e * d1
+            for t in range(TILES):
+                mask = lane < ends_at[t] - move
+                if e < 0 and t == 0:
+                    mask = mask & (lane >= -move)
+                value = left * band[q + 16 + move, :, t * LANES : (t + 1) * LANES]
+                px[e + 2, q, :, t * LANES : (t + 1) * LANES] = jnp.where(
+                    mask, value, 0.0
+                ).astype(jnp.bfloat16)
+
+    def loop(start, count, unroll, body, init=None):
         if init is None:
             def step(s, _):
                 for u in range(unroll):
@@ -106,21 +116,11 @@
             return carry
         return lax.fori_loop(0, count // unroll, step, init)
 
-    loop(0, 96, pair_row)
-
-    lane512 = lax.broadcasted_iota(jnp.int32, (16, OFF), 1)
-
-    def hidden_row(q, carry):
-        g_acc, a_acc = carry
-        stack = jnp.concatenate(
-            [px[b - a + 2, q + a * d1] for a in TAPS for b in TAPS], axis=0
-        )
-        mask = lane512 < reach[q]
-        first = jnp.where(mask, jnp.dot(w1[...], stack, preferred_element_type=jnp.float32), 0.0)
-        cdf = 0.5 * (1.0 + lax.erf(first * INV_ROOT_TWO))
-        slope = cdf + first * jnp.exp(-0.5 * first * first) * INV_ROOT_TWO_PI
-        hidden = (first * cdf).astype(jnp.bfloat16)
-        vstack = jnp.concatenate(
+    loop(0, 128, unroll, band_row)
+    loop(0, 96, unroll, pair_row)
+
+    def tap_rows(q):
+        return jnp.concatenate(
             [
                 jnp.concatenate(
                     [vga[t, pl.ds(pl.multiple_of((q - a * d2) * 8, 8), 8), :] for a in TAPS], axis=0
@@ -129,51 +129,63 @@
             ],
             axis=1,
         ).astype(jnp.bfloat16)
-        both = jnp.dot(vm[...], vstack, preferred_element_type=jnp.float32)
-        grad_hidden = both[:16] + both[16:]
+
+    def hidden_dots(q):
+        stack = jnp.concatenate(
+            [px[b - a + 2, q + a * d1] for a in TAPS for b in TAPS], axis=0
+        )
+        first = jnp.dot(w1[...], stack, preferred_element_type=jnp.float32)
+        return first, jnp.dot(vm[...], tap_rows(q), preferred_element_type=jnp.float32)
+
+    def hidden_values(q, first, grad_hidden):
+        mask = jnp.concatenate(masks(q), axis=1)
+        first = jnp.where(mask, first, 0.0)
+        cdf = 0.5 * (1.0 + lax.erf(first * INV_ROOT_TWO))
+        slope = cdf + first * jnp.exp(-0.5 * first * first) * INV_ROOT_TWO_PI
+        hidden = (first * cdf).astype(jnp.bfloat16)
         gf = jnp.where(mask, slope * grad_hidden, 0.0).astype(jnp.bfloat16)
         tiles = [gf[:, t * LANES : (t + 1) * LANES] for t in range(TILES)]
         for e in range(-2, 3):
             for t, tile in enumerate(shift_tiles(tiles, e, d1)):
                 gy[e + 2, q, :, t * LANES : (t + 1) * LANES] = tile
+        hid[q] = hidden
+        return hidden
+
+    def head_dot(q, hidden):
         hp = jnp.concatenate([hidden, px[2, q]], axis=0)
         zz = jnp.dot(zw[...], hp, preferred_element_type=jnp.float32)
-        zz = zz[:16] + zz[16:]
         for t in range(TILES):
             z[t, pl.ds(pl.multiple_of(q * 16, 16), 16), :] = zz[:, t * LANES : (t + 1) * LANES]
-        own = jnp.where((q >= 16) & (q < 80), 1.0, 0.0).astype(jnp.float32)
-        last = (((1,), (1,)), ((), ()))
-        g_acc = g_acc + own * lax.dot_general(gf, stack, last, preferred_element_type=jnp.float32)
-        a_acc = a_acc + own * lax.dot_general(vstack, hp, last, preferred_element_type=jnp.float32)
-        return g_acc, a_acc
-
-    g_acc, a_acc = loop(
-        8, 80, hidden_row, (jnp.zeros((16, 144), jnp.float32), jnp.zeros((24, 32), jnp.float32))
-    )
-    gconv[...] = jnp.zeros((16, 256), jnp.float32)
-    gconv[:, :144] = g_acc
-    acc[...] = jnp.zeros((24, LANES), jnp.float32)
-    acc[:, :32] = a_acc
-
-    lg[...] = jnp.zeros((16, LANES), jnp.float32)
-    rg[...] = jnp.zeros((16, 5 * LANES), jnp.float32)
+
+    def hidden_rows(s, _):
+        rows = [8 + s * unroll + u for u in range(unroll)]
+        dots, values = {}, {}
+        for u in range(unroll + lag + lag2):
+            if u < unroll:
+                dots[u] = hidden_dots(rows[u])
+            if 0 <= u - lag < unroll:
+                values[u - lag] = hidden_values(rows[u - lag], *dots.pop(u - lag))
+            if 0 <= u - lag - lag2:
+                head_dot(rows[u - lag - lag2], values.pop(u - lag - lag2))
+        return 0
+
+    lax.fori_loop(0, 80 // unroll, hidden_rows, 0)
 
     def grad_row(q, carry):
-        lg_acc, rg_acc = carry
+        lg_acc, rg_acc, w_acc = carry
         rr = q - 16
         stack = jnp.concatenate(
             [gy[b - a + 2, q - a * d1] for a in TAPS for b in TAPS], axis=0
         )
         grad_pair = jnp.dot(w1t[...], stack, preferred_element_type=jnp.float32)
-        n = reach[q]
-        left = pltpu.roll(lb[...], lax.rem(LANES - q, LANES), 1)[:, 0:1]
+        left = lcol[q]
         prods = []
         spread = []
-        for t in range(TILES):
+        for t, mask in enumerate(masks(q)):
             cols = slice(t * LANES, (t + 1) * LANES)
             g = vga[t, pl.ds(q * 8 + 2, 1), :]
-            gp = jnp.where(lane + t * LANES < n, grad_pair[:, cols] + head[...] * g, 0.0)
-            prods.append(gp * band[q, :, cols])
+            gp = jnp.where(mask, grad_pair[:, cols] + head[...] * g, 0.0)
+            prods.append(gp * band[q + 16, :, cols])
             spread.append(pltpu.roll(gp * left, rr, 1))
         total = (prods[0] + prods[1]) + (prods[2] + prods[3])
         lg_acc = jnp.where(lane == rr, jnp.sum(total, axis=1, keepdims=True), lg_acc)
@@ -183,13 +195,26 @@
         rg_acc = tuple(
             r + jnp.where(lane < rr, b, a) for r, b, a in zip(rg_acc, before, after)
         )
-        return lg_acc, rg_acc
+        w_acc = w_acc + lax.dot_general(
+            jnp.concatenate([stack, tap_rows(q)], axis=0),
+            jnp.concatenate([px[2, q], hid[q]], axis=0),
+            (((1,), (1,)), ((), ())),
+            preferred_element_type=jnp.float32,
+        )
+        return lg_acc, rg_acc, w_acc
 
     zero = jnp.zeros((16, LANES), jnp.float32)
-    lg_acc, rg_acc = loop(16, 64, grad_row, (zero, (zero,) * (TILES + 1)))
+    lg_acc, rg_acc, w_acc = loop(
+        16, 64, unroll3, grad_row, (zero, (zero,) * (TILES + 1), jnp.zeros((168, 32), jnp.float32))
+    )
     lg[...] = lg_acc
     for t in range(TILES + 1):
         rg[:, t * LANES : (t + 1) * LANES] = rg_acc[t]
+    acc[...] = jnp.zeros((256, LANES), jnp.float32)
+    acc[:168, :32] = w_acc
+    turned = acc[...].T
+    gconv[...] = turned[:16]
+    taps[...] = turned[16:32, LANES:]
 
     def zrows(t, a, row):
         return z[t, pl.ds((16 + a * d2) * 16 + row, 64, stride=16), :]
@@ -213,10 +238,6 @@
     w1 = first_w.reshape(16, 144)
     w1t = jnp.transpose(first_w, (3, 1, 2, 0)).reshape(16, 144)
     v = jnp.sum(second_w.astype(jnp.float32) * head[:, None, None, None], axis=0)
-    def split(m):
-        hi = m.astype(jnp.bfloat16)
-        lo = (m - hi.astype(jnp.float32)).astype(jnp.bfloat16)
-        return jnp.concatenate([hi, lo], axis=0)
     vt = jnp.transpose(v, (2, 0, 1))
     vm = jnp.concatenate(
         [jnp.pad(vt[:, a], ((0, 0), (2 - a, 3 + a))) for a in range(3)], axis=1
@@ -229,31 +250,34 @@
         ],
         axis=0,
     )
-    return w1, w1t, split(vm), split(zw)
-
-
-def local_call(ends, dil, rb, lb, cot96, w1, w1t, vm, zw, head_col, unroll=2):
+    return w1, w1t, vm.astype(jnp.bfloat16), zw.astype(jnp.bfloat16)
+
+
+def local_call(ends, dil, rb, lb, cot96, w1, w1t, vm, zw, head_col, unroll=8, unroll3=8, lag=3, lag2=2):
     v = pl.BlockSpec(memory_space=pltpu.VMEM)
     s = pl.BlockSpec(memory_space=pltpu.SMEM)
     f32 = jnp.float32
     return pl.pallas_call(
-        functools.partial(local_kernel, unroll=unroll),
+        functools.partial(local_kernel, unroll=unroll, unroll3=unroll3, lag=lag, lag2=lag2),
         out_shape=(
             jax.ShapeDtypeStruct((64, OFF), f32),
             jax.ShapeDtypeStruct((16, LANES), f32),
             jax.ShapeDtypeStruct((16, 5 * LANES), f32),
             jax.ShapeDtypeStruct((16, 256), f32),
-            jax.ShapeDtypeStruct((24, LANES), f32),
+            jax.ShapeDtypeStruct((16, LANES), f32),
         ),
         in_specs=[s, s] + [v] * 8,
         out_specs=[v] * 5,
         scratch_shapes=[
+            pltpu.VMEM((256, LANES), f32),
             pltpu.VMEM((5, 96, 16, OFF), jnp.bfloat16),
             pltpu.VMEM((5, 96, 16, OFF), jnp.bfloat16),
-            pltpu.VMEM((96, 16, OFF), f32),
+            pltpu.VMEM((96, 16, OFF), jnp.bfloat16),
+            pltpu.VMEM((128, 16, OFF), f32),
             pltpu.VMEM((TILES, 96 * 8, LANES), f32),
             pltpu.VMEM((TILES, 96 * 16, LANES), f32),
-            pltpu.SMEM((96,), jnp.int32),
+            pltpu.VMEM((TILES, 96, LANES), jnp.int32),
+            pltpu.VMEM((96, 16, LANES), f32),
         ],
         compiler_params=pltpu.CompilerParams(vmem_limit_bytes=52 * 1024 * 1024),
     )(ends, dil, rb, lb, cot96, w1, w1t, vm, zw, head_col)
@@ -313,11 +337,11 @@
     for c in rest:
         c.wait()
     for t in range(TILES + 1):
-        low = pltpu.roll(slots[2 * t], 80, 1)
-        mid = pltpu.roll(slots[2 * t + 1], 16, 1)
-        high = pltpu.roll(slots[2 * t + 2], 80, 1)
+        low = pltpu.roll(slots[2 * t], 96, 1)
+        mid = pltpu.roll(slots[2 * t + 1], 32, 1)
+        high = pltpu.roll(slots[2 * t + 2], 96, 1)
         rb[:, t * LANES : (t + 1) * LANES] = jnp.where(
-            lane < 16, low, jnp.where(lane < 80, mid, high)
+            lane < 32, low, jnp.where(lane < 96, mid, high)
         )
     lb[...] = jnp.where(
         lane < 16,
@@ -353,7 +377,7 @@
 
 
 def reduce_kernel(
-    scale, contact, rg, lg, gconv, acc, full, wt, wother,
+    scale, contact, rg, lg, gconv, taps, full, wt, wother,
     contacts, emb_grad, fin,
     csend, crecv, rsend, rrecv, lrsend, lrrecv, buf, arecv, brecv, send_sem, recv_sem,
 ):
@@ -406,8 +430,8 @@
         buf[j, 0:8, :] = wpart[8 * i : 8 * i + 8, t * LANES : (t + 1) * LANES]
         if j < 4:
             buf[j, 8:16, :] = gconv[8 * (j // 2) : 8 * (j // 2) + 8, (j % 2) * LANES : (j % 2 + 1) * LANES]
-        elif j < 7:
-            buf[j, 8:16, :] = acc[8 * (j - 4) : 8 * (j - 3), :]
+        elif j < 6:
+            buf[j, 8:16, :] = taps[8 * (j - 4) : 8 * (j - 3), :]
         else:
             buf[j, 8:16, :] = jnp.zeros((8, LANES), jnp.float32)
     stage = []
@@ -471,7 +495,7 @@
         ).wait_recv()
 
 
-def reduce_call(scale, contact, rg, lg, gconv, acc, full, wt, wother):
+def reduce_call(scale, contact, rg, lg, gconv, taps, full, wt, wother):
     v = pl.BlockSpec(memory_space=pltpu.VMEM)
     f32, bf16 = jnp.float32, jnp.bfloat16
     return pl.pallas_call(
@@ -499,7 +523,7 @@
         compiler_params=pltpu.CompilerParams(
             collective_id=1, has_side_effects=True, vmem_limit_bytes=16 * 1024 * 1024
         ),
-    )(contact, rg, lg, gconv, acc, full, wt, wother)
+    )(contact, rg, lg, gconv, taps, full, wt, wother)
 
 
 def on_device(
@@ -519,18 +543,19 @@
     full, rb, lb, cot96, wother = gather_call(embeddings, wt, cotangent)
     forms = weight_forms(first_conv_weight, second_conv_weight, head_weight)
     head_col = jnp.broadcast_to(head_weight[:, None], (16, LANES))
-    contact, lg, rg, gconv, acc = local_call(
+    contact, lg, rg, gconv, taps = local_call(
         chrom_ends, dilations, rb, lb, cot96, *forms, head_col
     )
     contacts, emb_grad, fin = reduce_call(
-        scale, contact, rg, lg, gconv, acc, full, wt, wother
+        scale, contact, rg, lg, gconv, taps, full, wt, wother
     )
     weights = jnp.transpose(fin[:, :8].reshape(4, 4, 8, LANES), (0, 2, 1, 3)).reshape(32, 512)
-    first_grad = jnp.transpose(fin[:4, 8:].reshape(2, 2, 8, LANES), (0, 2, 1, 3)).reshape(16, 256)
-    taps = fin[4:7, 8:]
-    moved = jnp.stack([taps[0, 2:5, :16], taps[1, 1:4, :16], taps[2, 0:3, :16]])
+    sums = jnp.transpose(fin[:4, 8:].reshape(2, 2, 8, LANES), (0, 2, 1, 3)).reshape(16, 256)
+    first_grad = jnp.transpose(sums[:, :144].reshape(16, 3, 3, 16), (3, 1, 2, 0))
+    shifts = fin[4:6, 8:].reshape(16, LANES)[:, 16:40].reshape(16, 3, 8)
+    moved = jnp.stack([shifts[:, 0, 2:5].T, shifts[:, 1, 1:4].T, shifts[:, 2, 0:3].T])
     second_grad = head_weight[:, None, None, None] * moved[None]
-    head_grad = taps[1, 2, 16:32] + jnp.sum(
+    head_grad = sums[:, 154] + jnp.sum(
         second_conv_weight.astype(jnp.float32) * moved[None], axis=(1, 2, 3)
     )
     return (
@@ -538,7 +563,7 @@
         emb_grad,
         weights[:16].T,
         weights[16:].T,
-        first_grad[:, :144].reshape(16, 3, 3, 16),
+        first_grad,
         second_grad,
         head_grad,
     )

time: 98.1 us -> 72.2 us (0.74)
  Pallas kernels: 87.8 us -> 62.2 us
    pallas_call x1, Pallas kernels: 43.9 us -> 18.2 us  [local_call(): pl.pallas_call(functools.partial(local_kernel, unroll=unroll, unroll3=unr...]
where the time goes in v2:
time: 72.2 us; the launch traced here: 71.9 us
  Pallas kernels  62.2 us (86%)
  local copies, waits for them, and re-layouts  6.62 us (9%)
  other arithmetic  2.37 us (3%)
  between operations  0.76 us (1%)
    pallas_call x1, Pallas kernels, reduce_call(): pl.pallas_call(functools.partial(reduce_kernel, scale), out_shape=(jax.Sh...  25.2 us
    pallas_call x1, Pallas kernels, gather_call(): pl.pallas_call(gather_kernel, out_shape=(jax.ShapeDtypeStruct((ROWS, 512)...  18.7 us
    pallas_call x1, Pallas kernels, local_call(): pl.pallas_call(functools.partial(local_kernel, unroll=unroll, unroll3=unr...  18.2 us
    unnamed x22, local copies, waits for them, and re-layouts  4.93 us

profile of v2, /device:TPU:1, one launch (start us, length us, event | category | flops | bytes accessed | tf_op | source)
XLA Modules:
  0.0 71.9 jit_solution(271534817344785558)
XLA Ops:
  0.6 0.6 copy-done.8
  1.3 0.1 pad.35.clone
  1.4 0.9 %fusion = bf16[3,3,16]{2,1,0:T(4,128)(2,1)S(1)} fusion(bf16[16,3,3,16]{3,0,2,1:T(8,128)(2,1)} %param.13, f32[16]{0:T(128)S(1)} %copy-done.8), kind=kLoop, calls=%fused_computation.2 | loop fusion | flops 6768 | bytes 4960 | tf_op jit(solution)/shard_map/reduce_sum | solution.py:240
  2.3 0.1 copy.32
  2.4 0.1 copy.34
  2.5 0.1 copy.33
  2.5 0.1 fusion.12.vm
  2.6 0.1 fusion.10.zw
  2.7 0.3 copy-done.5
  3.0 0.1 copy.37.w1t
  3.1 0.1 broadcast_in_dim.9.head
  3.1 0.6 copy-done.6
  3.7 0.0 copy-done.7
  3.8 0.0 copy-start.1
  3.8 0.1 reshape.48.w1
  3.9 0.7 copy-done
  4.6 18.7 %shard_map.144 = (bf16[64,512]{1,0:T(8,128)(2,1)S(1)}, f32[16,640]{1,0:T(8,128)S(1)}, f32[16,128]{1,0:T(8,128)S(1)}, bf16[96,512]{1,0:T(8,128)(2,1)S(1)}, bf16[32,256]{1,0:T(8,128)(2,1)S(1)}) custom-call(bf16[64,256]{1,0:T(8,128)(2,1)S(1)} %copy-done.1, bf16[32,512]{1,0:T(8,128)(2,1)S(1)} %pad_maximum_fusion.wt, bf16[64,512]{1,0:T(8,128)(2,1)S(1)} %copy-done), custom_call_target="tpu_custom_call" | custom-call | tf_op jit(solution)/shard_map/pallas_call | solution.py:357
  23.3 0.0 copy-start.2
  23.4 0.6 copy-done.2
  24.0 0.0 copy-done.3
  24.0 18.2 %shard_map.145 = (f32[64,512]{1,0:T(8,128)S(1)}, f32[16,128]{1,0:T(8,128)S(1)}, f32[16,640]{1,0:T(8,128)S(1)}, f32[16,256]{1,0:T(8,128)S(1)}, f32[16,128]{1,0:T(8,128)S(1)}) custom-call(s32[8]{0:T(128)S(1)} %copy-done.2, s32[2]{0:T(128)S(1)} %copy-done.3, f32[16,640]{1,0:T(8,128)S(1)} %get-tuple-element.20.rb, f32[16,128]{1,0:T(8,128)S(1)} %get-tuple-element.21.lb, ...), custom_call_target="tpu_custom_call" | custom-call | tf_op jit(solution)/shard_map/pallas_call | solution.py:260
  42.2 25.2 %shard_map.146 = (f32[64,512]{1,0:T(8,128)S(1)}, bf16[64,256]{1,0:T(8,128)(2,1)S(1)}, f32[16,16,128]{2,1,0:T(8,128)S(1)}) custom-call(f32[64,512]{1,0:T(8,128)S(1)} %get-tuple-element.23.contact, f32[16,640]{1,0:T(8,128)S(1)} %get-tuple-element.24.rg, f32[16,128]{1,0:T(8,128)S(1)} %get-tuple-element.25.lg, f32[16,256]{1,0:T(8,128)S(1)} %get-tuple-element.26.gconv, ...), custom_call_target="tpu_custom_call" | custom-call | tf_op jit(solution)/shard_map/pallas_call | solution.py:501
  67.4 0.1 slice.73
  67.5 0.1 copy.35
  67.7 0.6 slice_bitcast_fusion
  68.3 0.2 slice_reduce_fusion
  68.5 0.8 %fusion.1 = (f32[16]{0:T(128)S(1)}, f32[16,3,3,16]{3,0,2,1:T(8,128)}) fusion(bf16[16,3,3,16]{3,0,2,1:T(8,128)(2,1)S(1)} %copy-done.4, f32[3,3,16]{2,1,0:T(4,128)S(1)} %pad_maximum_fusion.1, f32[16]{0:T(128)S(1)} %copy-done.8), kind=kLoop, calls=%fused_computation.3 | loop fusion | flops 9200 | bytes 14528 | tf_op jit(solution)/shard_map/reduce_sum | solution.py:558
  69.3 0.5 add.13
  69.8 0.1 reshape.54
  69.9 0.7 %copy.36 = f32[16,3,3,16]{3,0,2,1:T(8,128)} copy(f32[16,3,3,16]{0,2,1,3:T(4,128)S(1)} %bitcast.53) | data formatting | bytes 18432
  70.6 0.7 copy.40
  71.3 0.6 copy.41
  (20 shorter events, 0.1 us)
Async XLA Ops:
  0.6 0.7 copy-start.8
  2.2 0.8 %copy-start.5 = (bf16[16,3,3,16]{3,0,2,1:T(8,128)(2,1)S(1)}, bf16[16,3,3,16]{3,0,2,1:T(8,128)(2,1)}, u32[]{:S(2)}) copy-start(bf16[16,3,3,16]{3,0,2,1:T(8,128)(2,1)} %param.12) | copy-start | bytes 13828
  3.0 0.7 copy-start.6
  3.0 0.7 %copy-start.7 = (bf16[512,16]{0,1:T(8,128)(2,1)S(1)}, bf16[512,16]{0,1:T(8,128)(2,1)}, u32[]{:S(2)}) copy-start(bf16[512,16]{0,1:T(8,128)(2,1)} %param.10) | copy-start | bytes 49156
  3.7 0.8 %copy-start = (bf16[64,512]{1,0:T(8,128)(2,1)S(1)}, bf16[64,512]{1,0:T(8,128)(2,1)}, u32[]{:S(2)}) copy-start(bf16[64,512]{1,0:T(8,128)(2,1)} %cot.1) | copy-start | bytes 196612
  3.8 0.8 %copy-start.1 = (bf16[64,256]{1,0:T(8,128)(2,1)S(1)}, bf16[64,256]{1,0:T(8,128)(2,1)}, u32[]{:S(2)}) copy-start(bf16[64,256]{1,0:T(8,128)(2,1)} %emb.1) | copy-start | bytes 98308
  23.3 0.7 copy-start.2
  23.4 0.7 copy-start.3
  67.6 0.8 %copy-start.4 = (bf16[16,3,3,16]{3,0,2,1:T(8,128)(2,1)S(1)}, bf16[16,3,3,16]{3,0,2,1:T(8,128)(2,1)}, u32[]{:S(2)}) copy-start(bf16[16,3,3,16]{3,0,2,1:T(8,128)(2,1)} %param.13) | copy-start | bytes 13828

commit v3 on v0

v3 whole, which is shorter than its diff:
```python
import functools
import math

import jax
import jax.numpy as jnp
from jax import lax
from jax.experimental import pallas as pl
from jax.experimental.pallas import tpu as pltpu
from jax.sharding import PartitionSpec as P

MESH = pl.DeviceIdType.MESH
F32 = jnp.float32
BF16 = jnp.bfloat16
OFF = 512
LANES = 128
TILES = OFF // LANES
ROWS = 64
RIM = 16
SLAB = ROWS + 2 * RIM
REACH = OFF // ROWS
BEHIND = REACH + 1
TAPS = (-1, 0, 1)
BATCH = 8
GROUP = 16
PLANES = 8
INV_ROOT_TWO = 0.7071067811865476
INV_ROOT_TWO_PI = 0.3989422804014327
LAST = (((1,), (1,)), ((), ()))
FIRST = (((0,), (0,)), ((), ()))


def ids(shape, dim):
    return lax.broadcasted_iota(jnp.int32, shape, dim)


def dot(a, b, dims=(((1,), (0,)), ((), ()))):
    return lax.dot_general(a, b, dims, preferred_element_type=F32)


def cols(t):
    return slice(t * LANES, (t + 1) * LANES)


def hop(me, distance):
    count = lax.axis_size("chrom")
    return lax.rem(me + distance + count, count)


def shift_tiles(tiles, count, dist):
    if count == 0:
        return tiles
    lane = ids((tiles[0].shape[0], LANES), 1)
    zero = jnp.zeros_like(tiles[0])
    if count > 0:
        amount = count * dist
        rolled = [pltpu.roll(t, amount, 1) for t in tiles]
        before = [zero] + rolled[:-1]
        return [jnp.where(lane < amount, b, r) for b, r in zip(before, rolled)]
    amount = LANES + count * dist
    rolled = [pltpu.roll(t, amount, 1) for t in tiles]
    after = rolled[1:] + [zero]
    return [jnp.where(lane < amount, r, a) for r, a in zip(rolled, after)]


def diagonal(column, lanes):
    shape = (16, lanes)
    return jnp.sum(jnp.where(ids(shape, 0) == ids(shape, 1), column, 0.0), axis=0, keepdims=True)


def head_column(head, lanes):
    sub = ids((16, lanes), 0)
    column = jnp.zeros((16, lanes), F32)
    for o in range(16):
        column = jnp.where(sub == o, head[o], column)
    return column


def band_kernel(
    scale,
    ends, dil, head, emb, w_left, w_right, first_w, second_w, cot,
    contacts, emb_grad, fin,
    wt, wother, w1, w1t, vm, zw,
    full, ahead, slots, cot96, rb, lb, lcol, edge, vga, band, px, gy, hid, z, zs, acc,
    csend, crecv, rsend, rrecv, lrsend, lrrecv, buf, arecv, brecv,
    send_sem, recv_sem, plane_send, plane_recv, last_send, last_recv,
):
    me = lax.axis_index("chrom")
    half = lax.axis_index("chan")
    other = 1 - half
    place = lax.rem(me, GROUP)
    plane = me // GROUP
    base = me - place
    mine = pl.ds(pl.multiple_of(half * 256, 256), 256)
    theirs = pl.ds(pl.multiple_of(other * 256, 256), 256)
    d1 = dil[0]
    d2 = dil[1]
    lane = ids((16, LANES), 1)

    barrier = pltpu.get_barrier_semaphore()
    sources = [(hop(me, d), half) for d in range(1, BEHIND + 1)]
    sources += [(hop(me, -d), half) for d in range(1, REACH + 1)]
    sources += [(base + lax.rem(place + s, GROUP), half) for s in range(1, GROUP)]
    sources += [(lax.rem(plane + s, PLANES) * GROUP + place, half) for s in range(1, PLANES)]
    sources += [(me, other)]
    for chrom, chan in sources:
        pl.semaphore_signal(
            barrier, inc=1, device_id={"chrom": chrom, "chan": chan}, device_id_type=MESH
        )

    def copy(index, src, dst, chrom, chan):
        c = pltpu.make_async_remote_copy(
            src_ref=src, dst_ref=dst, send_sem=send_sem.at[index], recv_sem=recv_sem.at[index],
            device_id={"chrom": chrom, "chan": chan}, device_id_type=MESH,
        )
        c.start()
        return c

    full[:, mine] = emb[...]
    wt[0:16, :] = w_left[...]
    wt[16:32, :] = w_right[...]
    cot96[RIM : RIM + ROWS, :] = cot[...]
    pl.semaphore_wait(barrier, len(sources))

    emb_copy = copy(0, emb, full.at[:, mine], me, other)
    rims = [
        copy(1, cot.at[pl.ds(ROWS - RIM, RIM)], cot96.at[pl.ds(0, RIM)], hop(me, 1), half),
        copy(2, cot.at[pl.ds(0, RIM)], cot96.at[pl.ds(RIM + ROWS, RIM)], hop(me, -1), half),
    ]
    w_copy = copy(3, wt.at[:, theirs], wother, me, other)

    head16 = head_column(head, 16)
    sub16 = ids((16, 16), 0)
    rows = jnp.zeros((16, 16), F32)
    form = jnp.zeros((16, 144), F32)
    form_t = jnp.zeros((16, 144), F32)
    for ab in range(9):
        at = (ids((16, 144), 1) == ids((16, 144), 0) + 16 * ab).astype(BF16)
        form = form + dot(first_w[ab], at)
        form_t = form_t + dot(first_w[ab], at, FIRST)
        row = jnp.sum(head16 * second_w[ab].astype(F32), axis=0, keepdims=True)
        rows = jnp.where(sub16 == ab, row, rows)
    w1[...] = form.astype(BF16)
    w1t[...] = form_t.astype(BF16)
    head_rows = jnp.where(sub16 == 9, diagonal(head16, 16), 0.0).astype(BF16)
    rows = rows.astype(BF16)
    low = (ids((16, 32), 1) == ids((16, 32), 0)).astype(BF16)
    high = (ids((16, 32), 1) == ids((16, 32), 0) + 16).astype(BF16)
    zw[...] = (dot(rows, low) + dot(head_rows, high)).astype(BF16)
    tap = ids((16, 24), 0)
    column = tap + 4 * ((tap >= 3).astype(jnp.int32) + (tap >= 6).astype(jnp.int32)) + 2
    spot = ((ids((16, 24), 1) == column) & (tap < 9)).astype(BF16)
    vm[...] = dot(rows, spot, FIRST).astype(BF16)

    emb_copy.wait_recv()
    twice = jnp.concatenate([full[...], full[...]], axis=0)
    slots[1] = jnp.where(lane < ROWS, dot(wt[16:32, :], twice, LAST), dot(wt[0:16, :], twice, LAST))
    tiles = [
        copy(3 + d, slots.at[1], slots.at[1 + d], hop(me, -d), half)
        for d in range(1, BEHIND + 1)
    ]
    tiles.append(copy(4 + BEHIND, slots.at[1], slots.at[0], hop(me, 1), half))
    ahead[0] = full[...]
    spread_copies = [
        copy(4 + BEHIND + d, full, ahead.at[d], hop(me, -d), half)
        for d in range(1, REACH + 1)
    ]

    for c in rims:
        c.wait()
    big = jnp.int32(1 << 30)
    bins = ids((SLAB, LANES), 0) + (me * ROWS - RIM)
    stop = jnp.full((SLAB, LANES), big)
    for j in range(8):
        stop = jnp.minimum(stop, jnp.where(ends[j] > bins, ends[j], big))
    width = jnp.where((bins >= 0) & (stop < big), jnp.minimum(stop - bins, OFF), 0)
    slab_lane = ids((SLAB, LANES), 1)
    masked = []
    for t in range(TILES):
        edge[t] = width - t * LANES
        masked.append(
            jnp.where(slab_lane < width - t * LANES, cot96[:, cols(t)].astype(F32), 0.0)
        )
    for e in range(-2, 3):
        for t, tile in enumerate(shift_tiles(masked, e, d2)):
            vga[:, t, e + 2, :] = tile
    for e in range(5, 8):
        for t in range(TILES):
            vga[:, t, e, :] = jnp.zeros((SLAB, LANES), F32)

    for c in tiles:
        c.wait()
    for t in range(TILES + 1):
        before = pltpu.roll(slots[2 * t], 96, 1)
        inside = pltpu.roll(slots[2 * t + 1], 32, 1)
        after = pltpu.roll(slots[2 * t + 2], 96, 1)
        rb[:, cols(t)] = jnp.where(lane < 32, before, jnp.where(lane < 96, inside, after))
    lb[...] = jnp.where(
        lane < RIM,
        pltpu.roll(slots[0], 16, 1),
        jnp.where(lane < RIM + ROWS, pltpu.roll(slots[1], 80, 1), pltpu.roll(slots[2], 16, 1)),
    )
    for q in range(SLAB):
        lcol[q] = jnp.broadcast_to(lb[:, q : q + 1], (16, LANES))

    def masks(q):
        return [lane < edge[t, pl.ds(q, 1), :] for t in range(TILES)]

    def band_rows(s, _):
        for u in range(BATCH):
            p = s * BATCH + u
            back = lax.rem(LANES - p, LANES)
            rolled = [pltpu.roll(rb[:, cols(t)], back, 1) for t in range(TILES + 1)]
            for t in range(TILES):
                band[p, :, cols(t)] = jnp.where(lane < LANES - p, rolled[t], rolled[t + 1])
        return 0

    lax.fori_loop(0, (SLAB + 2 * RIM) // BATCH, band_rows, 0)

    def pair_rows(s, _):
        for u in range(BATCH):
            q = s * BATCH + u
            left = lcol[q]
            limits = [edge[t, pl.ds(q, 1), :] for t in range(TILES)]
            for e in range(-2, 3):
                move = e * d1
                for t in range(TILES):
                    mask = lane < limits[t] - move
                    if e < 0 and t == 0:
                        mask = mask & (lane >= -move)
                    value = left * band[q + RIM + move, :, cols(t)]
                    px[e + 2, q, :, cols(t)] = jnp.where(mask, value, 0.0).astype(BF16)
        return 0

    lax.fori_loop(0, SLAB // BATCH, pair_rows, 0)

    def tap_rows(q):
        return jnp.concatenate(
            [
                jnp.concatenate([vga[q - a * d2, t] for a in TAPS], axis=0)
                for t in range(TILES)
            ],
            axis=1,
        ).astype(BF16)

    def hidden_dots(q):
        stack = jnp.concatenate([px[b - a + 2, q + a * d1] for a in TAPS for b in TAPS], axis=0)
        return dot(w1[...], stack), dot(vm[...], tap_rows(q))

    def hidden_values(q, first, grad_hidden):
        mask = jnp.concatenate(masks(q), axis=1)
        first = jnp.where(mask, first, 0.0)
        cdf = 0.5 * (1.0 + lax.erf(first * INV_ROOT_TWO))
        slope = cdf + first * jnp.exp(-0.5 * first * first) * INV_ROOT_TWO_PI
        hidden = (first * cdf).astype(BF16)
        grad_first = jnp.where(mask, slope * grad_hidden, 0.0).astype(BF16)
        parts = [grad_first[:, cols(t)] for t in range(TILES)]
        for e in range(-2, 3):
            for t, tile in enumerate(shift_tiles(parts, e, d1)):
                gy[e + 2, q, :, cols(t)] = tile
        hid[q] = hidden
        return hidden

    def head_dot(q, hidden):
        out = dot(zw[...], jnp.concatenate([hidden, px[2, q]], axis=0))
        for t in range(TILES):
            z[q, t] = out[:, cols(t)]

    def hidden_rows(s, _):
        lag, more = 3, 2
        dots, values = {}, {}
        for u in range(BATCH + lag + more):
            q = RIM // 2 + s * BATCH + u
            if u < BATCH:
                dots[u] = hidden_dots(q)
            if 0 <= u - lag < BATCH:
                values[u - lag] = hidden_values(q - lag, *dots.pop(u - lag))
            if u >= lag + more:
                head_dot(q - lag - more, values.pop(u - lag - more))
        return 0

    lax.fori_loop(0, (ROWS + RIM) // BATCH, hidden_rows, 0)

    def grad_rows(s, carry):
        for u in range(BATCH):
            carry = grad_row(s * BATCH + u, carry)
        return carry

    head_full = head_column(head, LANES)

    def grad_row(row, carry):
        left_acc, right_acc, weight_acc = carry
        q = row + RIM
        stack = jnp.concatenate([gy[b - a + 2, q - a * d1] for a in TAPS for b in TAPS], axis=0)
        grad_pair = dot(w1t[...], stack)
        left = lcol[q]
        prods, spread = [], []
        for t, mask in enumerate(masks(q)):
            g = vga[q, t, 2:3, :]
            part = jnp.where(mask, grad_pair[:, cols(t)] + head_full * g, 0.0)
            prods.append(part * band[q + RIM, :, cols(t)])
            spread.append(pltpu.roll(part * left, row, 1))
        total = (prods[0] + prods[1]) + (prods[2] + prods[3])
        left_acc = jnp.where(lane == row, jnp.sum(total, axis=1, keepdims=True), left_acc)
        zero = jnp.zeros((16, LANES), F32)
        right_acc = tuple(
            r + jnp.where(lane < row, b, a)
            for r, b, a in zip(right_acc, [zero] + spread, spread + [zero])
        )
        weight_acc = weight_acc + dot(
            jnp.concatenate([stack, tap_rows(q)], axis=0),
            jnp.concatenate([px[2, q], hid[q]], axis=0),
            LAST,
        )
        return left_acc, right_acc, weight_acc

    zero = jnp.zeros((16, LANES), F32)
    left_grad, right_terms, weight_acc = lax.fori_loop(
        0, ROWS // BATCH, grad_rows, (zero, (zero,) * (TILES + 1), jnp.zeros((168, 32), F32))
    )

    for d in range(1, REACH + 1):
        piece = right_terms[d // 2]
        rsend[d] = pltpu.roll(piece, ROWS, 1) if d % 2 else piece
    first_copy = 5 + BEHIND + REACH
    rights = [
        copy(first_copy + d, rsend.at[d], rrecv.at[d], hop(me, d), half)
        for d in range(1, REACH + 1)
    ]

    for c in spread_copies:
        c.wait()
    left_low = left_grad.astype(BF16)
    left_part = dot(left_low[:, :ROWS], ahead[0])
    right_part = jnp.zeros((16, OFF), F32)
    for t in range(TILES):
        pair_of = jnp.concatenate([ahead[2 * t], ahead[2 * t + 1]], axis=0)
        right_part = right_part + dot(right_terms[t].astype(BF16), pair_of)
    right_part = right_part + dot(right_terms[TILES][:, :ROWS].astype(BF16), ahead[REACH])
    acc[...] = jnp.zeros((256, LANES), F32)
    acc[:168, :32] = weight_acc
    turned = acc[...].T
    for j in range(GROUP):
        part = left_part if j < 8 else right_part
        r = 8 * ((j // 4) % 2)
        buf[j, 0:8, :] = part[r : r + 8, cols(j % 4)]
        if j < 4:
            r = 8 * (j // 2)
            buf[j, 8:16, :] = turned[r : r + 8, cols(j % 2)]
        elif j < 6:
            r = 8 * (j - 2)
            buf[j, 8:16, :] = turned[r : r + 8, cols(1)]
        else:
            buf[j, 8:16, :] = jnp.zeros((8, LANES), F32)
    group_copy = first_copy + REACH
    stage = []
    for s in range(1, GROUP):
        target = lax.rem(place + s, GROUP)
        stage.append(copy(group_copy + s, buf.at[target], arecv.at[s], base + target, half))

    def align_rows(s, _):
        for u in range(BATCH):
            row = s * BATCH + u
            for n, a in enumerate(TAPS):
                for t in range(TILES):
                    zs[n, t, pl.ds(pl.multiple_of(row * 16, 16), 16), :] = z[row + RIM + a * d2, t]
        return 0

    lax.fori_loop(0, ROWS // BATCH, align_rows, 0)

    def tap_sum(t, a, row):
        return zs[a + 1, t, pl.ds(row, ROWS, stride=16), :]

    total = None
    for e in range(-2, 3):
        parts = [
            sum(tap_sum(t, a, (a + 1) * 3 + a + e + 1) for a in TAPS if -1 <= a + e <= 1)
            for t in range(TILES)
        ]
        parts = shift_tiles(parts, -e, d2)
        total = parts if total is None else [x + y for x, y in zip(total, parts)]
    own_lane = ids((ROWS, LANES), 1)
    for t in range(TILES):
        second = jnp.where(own_lane < edge[t, RIM : RIM + ROWS, :], total[t], 0.0)
        csend[:, cols(t)] = (tap_sum(t, 0, 9) + second).astype(BF16)
    swap_copy = group_copy + GROUP
    swap = copy(swap_copy, csend, crecv, me, other)

    for c in rights:
        c.wait()
    right = right_terms[0]
    for d in range(1, REACH + 1):
        right = right + rrecv[d]
    right = jnp.where(lane < ROWS, right, 0.0)
    lrsend[...] = jnp.concatenate([left_low, right.astype(BF16)], axis=0)
    trade = copy(swap_copy + 1, lrsend, lrrecv, me, other)

    total = buf[place]
    for s, c in enumerate(stage):
        c.wait()
        total = total + arecv[s + 1]
    brecv[plane] = total

    def plane_copy(s, index, target):
        return pltpu.make_async_remote_copy(
            src_ref=brecv.at[index], dst_ref=brecv.at[index],
            send_sem=plane_send.at[s], recv_sem=plane_recv.at[index],
            device_id={"chrom": target * GROUP + place, "chan": half}, device_id_type=MESH,
        )

    planes = [(s, lax.rem(plane + s, PLANES)) for s in range(1, PLANES)]
    for s, p in planes:
        plane_copy(s, plane, p).start()

    emb_copy.wait_send()
    w_copy.wait()
    trade.wait()
    both = jnp.concatenate([lrsend[...], lrrecv[...]], axis=0)
    weights = jnp.concatenate([wt[:, mine], wother[...]], axis=0)
    emb_grad[...] = dot(both, weights, FIRST)[:ROWS].astype(BF16)
    swap.wait()
    contacts[...] = csend[...].astype(F32) + crecv[...].astype(F32)

    for s, p in planes:
        plane_copy(s, plane, p).wait_send()
        plane_copy(s, p, p).wait_recv()
    total = brecv[0]
    for p in range(1, PLANES):
        total = total + brecv[p]
    fin[place] = total * scale

    def last_copy(s, index, target):
        return pltpu.make_async_remote_copy(
            src_ref=fin.at[index], dst_ref=fin.at[index],
            send_sem=last_send.at[s], recv_sem=last_recv.at[index],
            device_id={"chrom": base + target, "chan": half}, device_id_type=MESH,
        )

    others = [(s, lax.rem(place + s, GROUP)) for s in range(1, GROUP)]
    for s, p in others:
        last_copy(s, place, p).start()
    for s, p in others:
        last_copy(s, place, p).wait_send()
        last_copy(s, p, p).wait_recv()


def band_call(scale, *operands):
    v = pl.BlockSpec(memory_space=pltpu.VMEM)
    m = pl.BlockSpec(memory_space=pltpu.SMEM)
    copies = 4 + BEHIND + REACH + 1 + REACH + GROUP + 4
    dma = pltpu.SemaphoreType.DMA
    return pl.pallas_call(
        functools.partial(band_kernel, scale),
        out_shape=(
            jax.ShapeDtypeStruct((ROWS, OFF), F32),
            jax.ShapeDtypeStruct((ROWS, 256), BF16),
            jax.ShapeDtypeStruct((GROUP, 16, LANES), F32),
        ),
        in_specs=[m] * 3 + [v] * 6,
        out_specs=[v] * 3,
        scratch_shapes=[
            pltpu.VMEM((32, 512), BF16),
            pltpu.VMEM((32, 256), BF16),
            pltpu.VMEM((16, 144), BF16),
            pltpu.VMEM((16, 144), BF16),
            pltpu.VMEM((16, 24), BF16),
            pltpu.VMEM((16, 32), BF16),
            pltpu.VMEM((ROWS, 512), BF16),
            pltpu.VMEM((REACH + 1, ROWS, 512), BF16),
            pltpu.VMEM((BEHIND + 2, 16, LANES), F32),
            pltpu.VMEM((SLAB, OFF), BF16),
            pltpu.VMEM((16, OFF + LANES), F32),
            pltpu.VMEM((16, LANES), F32),
            pltpu.VMEM((SLAB, 16, LANES), F32),
            pltpu.VMEM((TILES, SLAB, LANES), jnp.int32),
            pltpu.VMEM((SLAB, TILES, 8, LANES), F32),
            pltpu.VMEM((SLAB + 2 * RIM, 16, OFF), F32),
            pltpu.VMEM((5, SLAB, 16, OFF), BF16),
            pltpu.VMEM((5, SLAB, 16, OFF), BF16),
            pltpu.VMEM((SLAB, 16, OFF), BF16),
            pltpu.VMEM((SLAB, TILES, 16, LANES), F32),
            pltpu.VMEM((3, TILES, ROWS * 16, LANES), F32),
            pltpu.VMEM((256, LANES), F32),
            pltpu.VMEM((ROWS, OFF), BF16),
            pltpu.VMEM((ROWS, OFF), BF16),
            pltpu.VMEM((REACH + 1, 16, LANES), F32),
            pltpu.VMEM((REACH + 1, 16, LANES), F32),
            pltpu.VMEM((32, LANES), BF16),
            pltpu.VMEM((32, LANES), BF16),
            pltpu.VMEM((GROUP, 16, LANES), F32),
            pltpu.VMEM((GROUP, 16, LANES), F32),
            pltpu.VMEM((PLANES, 16, LANES), F32),
            dma((copies,)),
            dma((copies,)),
            dma((PLANES,)),
            dma((PLANES,)),
            dma((GROUP,)),
            dma((GROUP,)),
        ],
        compiler_params=pltpu.CompilerParams(
            collective_id=0, has_side_effects=True, vmem_limit_bytes=56 * 1024 * 1024
        ),
    )(*operands)


def output_kernel(
    head, fin, second_w, contacts_in, emb_grad_in,
    contacts, emb_grad, left_grad, right_grad, first_grad, second_grad, head_grad, wide,
):
    contacts[...] = contacts_in[...]
    emb_grad[...] = emb_grad_in[...]
    for j in range(GROUP):
        out = left_grad if j < 8 else right_grad
        r = 8 * ((j // 4) % 2)
        out[r : r + 8, cols(j % 4)] = fin[j, 0:8, :]
    wide[...] = jnp.zeros((LANES, 3 * LANES), F32)
    for j in range(4):
        r = 8 * (j // 2)
        wide[r : r + 8, cols(j % 2)] = fin[j, 8:16, :]
    wide[0:8, cols(2)] = fin[4, 8:16, :]
    wide[8:16, cols(2)] = fin[5, 8:16, :]
    turned = wide[...].T
    head_sum = wide[0:16, 154:155]
    head16 = head_column(head, 16)
    sums = jnp.zeros((16, 16), F32)
    for ab in range(9):
        a, b = ab // 3, ab % 3
        first_grad[ab] = turned[16 * ab : 16 * ab + 16, :16]
        row = 2 * LANES + 16 + 8 * a + (b - a + 2)
        moved = turned[row : row + 1, :16]
        second_grad[ab] = head16 * moved
        sums = sums + second_w[ab].astype(F32) * moved
    total = head_sum + jnp.sum(sums, axis=1, keepdims=True)
    head_grad[...] = diagonal(jnp.broadcast_to(total, (16, 16)), 16)


def output_call(head, fin, second_w, contacts, emb_grad):
    v = pl.BlockSpec(memory_space=pltpu.VMEM)
    m = pl.BlockSpec(memory_space=pltpu.SMEM)
    return pl.pallas_call(
        output_kernel,
        out_shape=(
            jax.ShapeDtypeStruct((ROWS, OFF), F32),
            jax.ShapeDtypeStruct((ROWS, 256), BF16),
            jax.ShapeDtypeStruct((16, 512), F32),
            jax.ShapeDtypeStruct((16, 512), F32),
            jax.ShapeDtypeStruct((9, 16, 16), F32),
            jax.ShapeDtypeStruct((9, 16, 16), F32),
            jax.ShapeDtypeStruct((1, 16), F32),
        ),
        in_specs=[m] + [v] * 4,
        out_specs=[v] * 7,
        scratch_shapes=[pltpu.VMEM((LANES, 3 * LANES), F32)],
    )(head, fin, second_w, contacts, emb_grad)


def on_device(
    embeddings,
    w_left,
    w_right,
    first_conv_weight,
    second_conv_weight,
    head_weight,
    cotangent,
    dilations,
    chrom_ends,
):
    bin_total = embeddings.shape[0] * lax.axis_size("chrom")
    scale = 1.0 / math.sqrt(bin_total * OFF)
    first_w = jnp.transpose(first_conv_weight, (1, 2, 0, 3)).reshape(9, 16, 16)
    second_w = jnp.transpose(second_conv_weight, (1, 2, 0, 3)).reshape(9, 16, 16)
    contacts, emb_grad, fin = band_call(
        scale, chrom_ends, dilations, head_weight, embeddings, w_left.T, w_right.T,
        first_w, second_w, cotangent,
    )
    contacts, emb_grad, left_grad, right_grad, first_grad, second_grad, head_grad = output_call(
        head_weight, fin, second_w, contacts, emb_grad
    )
    return (
        contacts,
        emb_grad,
        left_grad.T,
        right_grad.T,
        jnp.transpose(first_grad.reshape(3, 3, 16, 16), (2, 0, 1, 3)),
        jnp.transpose(second_grad.reshape(3, 3, 16, 16), (2, 0, 1, 3)),
        head_grad.reshape(16),
    )


def solution(mesh):
    in_specs = (
        P("chrom", "chan"),
        P(None, "chan"),
        P(None, "chan"),
        P("chan", None, None, None),
        P("chan", None, None, None),
        P("chan"),
        P("chrom", None),
        P(),
        P(),
    )
    out_specs = (
        P("chrom", None),
        P("chrom", "chan"),
        P(None, "chan"),
        P(None, "chan"),
        P("chan", None, None, None),
        P("chan", None, None, None),
        P("chan"),
    )
    return jax.shard_map(
        on_device, mesh=mesh, in_specs=in_specs, out_specs=out_specs, check_vma=False
    )
```

time: 1240 us -> 67.1 us (0.05)
  waiting for transfers between devices: 995 us -> 0 us
  starting transfers between devices: 90.2 us -> 0 us
  Pallas kernels: 0 us -> 66.3 us
  local copies, waits for them, and re-layouts: 58 us -> 0 us
  matrix products: 29.8 us -> 0 us
  between operations: 29.3 us -> 0.64 us
  other arithmetic: 20.5 us -> 0 us
    psum x2 -> x0, waiting for transfers between devices: 981 us -> none  [the longest x1 963 us: on_device(): lax.psum((left_wpart, right_wpart, first_weight_gradient, second_weight_g...]
    ppermute x24 -> x0, starting transfers between devices: 90.1 us -> none  [the longest x16 66.9 us: from_behind(): return lax.ppermute(block, axis, route)]
    pallas_call x0 -> x2, Pallas kernels: none -> 66.3 us  [the longest x1 64.3 us: band_call(): pl.pallas_call(functools.partial(band_kernel, scale), out_shape=(jax.Shap...]
    dot_general x25 -> x0, matrix products: 29.8 us -> none  [the longest x6 9.58 us: convolution_transpose(): jnp.einsum('tc,tik->cik', tap_matrix, stacked, preferred_element_type=jnp...]
    dynamic_slice x4 -> x0, local copies, waits for them, and re-layouts: 21.7 us -> none  [window(): return lax.dynamic_slice(padded, starts, (padded.shape[0], row_count, OFF))]
    reduce_scatter x1 -> x0, waiting for transfers between devices: 13.9 us -> none  [on_device(): lax.psum_scatter(emb_part.astype(jnp.bfloat16), 'chan', scatter_dimension...]
  transfers between devices with their start and end apart: 27 -> 0, of which waited for: 4 -> 0; matrix products, arithmetic and copies ran while one was open for 6% -> 0% of each run, Pallas kernels for 0% -> 0%
where the time goes in v3:
time: 67.1 us; the launch traced here: 66.9 us
  Pallas kernels  66.3 us (99%)
    pallas_call x1, Pallas kernels, band_call(): pl.pallas_call(functools.partial(band_kernel, scale), out_shape=(jax.Shap...  64.3 us
    pallas_call x1, Pallas kernels, output_call(): pl.pallas_call(output_kernel, out_shape=(jax.ShapeDtypeStruct((ROWS, OFF)...  1.92 us

profile of v3, /device:TPU:1, one launch (start us, length us, event | category | flops | bytes accessed | tf_op | source)
XLA Modules:
  0.0 66.9 jit_solution(11848178148623269744)
XLA Ops:
  0.6 64.3 %shard_map.144 = (f32[64,512]{1,0:T(8,128)}, bf16[64,256]{1,0:T(8,128)(2,1)}, f32[16,16,128]{2,1,0:T(8,128)}) custom-call(s32[8]{0:T(128)} %ends.1, s32[2]{0:T(128)} %dil.1, f32[16]{0:T(128)} %head.3, bf16[64,256]{1,0:T(8,128)(2,1)} %emb.1, bf16[16,512]{1,0:T(8,128)(2,1)} %bitcast.20, bf16[16,512]{1,0:T(8,128)(2,1)} %bitcast.21, ...), custom_call_target="tpu_custom_call" | custom-call | tf_op jit(solution)/shard_map/pallas_call | solution.py:451
  65.0 1.9 %shard_map.145 = (f32[64,512]{1,0:T(8,128)}, bf16[64,256]{1,0:T(8,128)(2,1)}, f32[16,512]{1,0:T(8,128)}, f32[16,512]{1,0:T(8,128)}, f32[9,16,16]{2,1,0:T(8,128)}, /*index=5*/f32[9,16,16]{2,1,0:T(8,128)}, f32[1,16]{1,0:T(1,128)}) custom-call(f32[16]{0:T(128)} %head.3, f32[16,16,128]{2,1,0:T(8,128)} %get-tuple-element.17.fin, bf16[9,16,16]{2,1,0:T(8,128)(2,1)} %bitcast.18, ...), custom_call_target="tpu_custom_call" | custom-call | tf_op jit(solution)/shard_map/pallas_call | solution.py:539

commit v4 on v3

--- a/solution.py
+++ b/solution.py
@@ -77,12 +77,12 @@
 
 def band_kernel(
     scale,
-    ends, dil, head, emb, w_left, w_right, first_w, second_w, cot,
+    ends, dil, head, emb, w_left, w_right, first_in, second_in, cot,
     contacts, emb_grad, fin,
-    wt, wother, w1, w1t, vm, zw,
+    wt, wother, first_w, second_w, w1, w1t, vm, zw,
     full, ahead, slots, cot96, rb, lb, lcol, edge, vga, band, px, gy, hid, z, zs, acc,
     csend, crecv, rsend, rrecv, lrsend, lrrecv, buf, arecv, brecv,
-    send_sem, recv_sem, plane_send, plane_recv, last_send, last_recv,
+    load_sem, send_sem, recv_sem, plane_send, plane_recv, last_send, last_recv,
 ):
     me = lax.axis_index("chrom")
     half = lax.axis_index("chan")
@@ -115,10 +115,21 @@
         c.start()
         return c
 
-    full[:, mine] = emb[...]
-    wt[0:16, :] = w_left[...]
-    wt[16:32, :] = w_right[...]
-    cot96[RIM : RIM + ROWS, :] = cot[...]
+    loads = [
+        pltpu.make_async_copy(src, dst, load_sem.at[n])
+        for n, (src, dst) in enumerate(
+            [
+                (emb, full.at[:, mine]),
+                (w_left, wt.at[pl.ds(0, 16)]),
+                (w_right, wt.at[pl.ds(16, 16)]),
+                (first_in, first_w),
+                (second_in, second_w),
+                (cot, cot96.at[pl.ds(RIM, ROWS)]),
+            ]
+        )
+    ]
+    for load in loads:
+        load.start()
     pl.semaphore_wait(barrier, len(sources))
 
     emb_copy = copy(0, emb, full.at[:, mine], me, other)
@@ -126,6 +137,8 @@
         copy(1, cot.at[pl.ds(ROWS - RIM, RIM)], cot96.at[pl.ds(0, RIM)], hop(me, 1), half),
         copy(2, cot.at[pl.ds(0, RIM)], cot96.at[pl.ds(RIM + ROWS, RIM)], hop(me, -1), half),
     ]
+    for load in loads:
+        load.wait()
     w_copy = copy(3, wt.at[:, theirs], wother, me, other)
 
     head16 = head_column(head, 16)
@@ -160,9 +173,9 @@
     ]
     tiles.append(copy(4 + BEHIND, slots.at[1], slots.at[0], hop(me, 1), half))
     ahead[0] = full[...]
-    spread_copies = [
+    far_copies = [
         copy(4 + BEHIND + d, full, ahead.at[d], hop(me, -d), half)
-        for d in range(1, REACH + 1)
+        for d in range(2, REACH + 1, 2)
     ]
 
     for c in rims:
@@ -205,32 +218,36 @@
     def masks(q):
         return [lane < edge[t, pl.ds(q, 1), :] for t in range(TILES)]
 
-    def band_rows(s, _):
+    def band_row(p):
+        back = lax.rem(2 * LANES - p, LANES)
+        rolled = [pltpu.roll(rb[:, cols(t)], back, 1) for t in range(TILES + 1)]
+        for t in range(TILES):
+            band[p, :, cols(t)] = jnp.where(lane < LANES - p, rolled[t], rolled[t + 1])
+
+    def pair_row(q):
+        left = lcol[q]
+        limits = [edge[t, pl.ds(q, 1), :] for t in range(TILES)]
+        for e in range(-2, 3):
+            move = e * d1
+            for t in range(TILES):
+                mask = lane < limits[t] - move
+                if e < 0 and t == 0:
+                    mask = mask & (lane >= -move)
+                value = left * band[q + RIM + move, :, cols(t)]
+                px[e + 2, q, :, cols(t)] = jnp.where(mask, value, 0.0).astype(BF16)
+
+    def first_band_rows(s, _):
         for u in range(BATCH):
-            p = s * BATCH + u
-            back = lax.rem(LANES - p, LANES)
-            rolled = [pltpu.roll(rb[:, cols(t)], back, 1) for t in range(TILES + 1)]
-            for t in range(TILES):
-                band[p, :, cols(t)] = jnp.where(lane < LANES - p, rolled[t], rolled[t + 1])
+            band_row(s * BATCH + u)
         return 0
-
-    lax.fori_loop(0, (SLAB + 2 * RIM) // BATCH, band_rows, 0)
 
     def pair_rows(s, _):
         for u in range(BATCH):
-            q = s * BATCH + u
-            left = lcol[q]
-            limits = [edge[t, pl.ds(q, 1), :] for t in range(TILES)]
-            for e in range(-2, 3):
-                move = e * d1
-                for t in range(TILES):
-                    mask = lane < limits[t] - move
-                    if e < 0 and t == 0:
-                        mask = mask & (lane >= -move)
-                    value = left * band[q + RIM + move, :, cols(t)]
-                    px[e + 2, q, :, cols(t)] = jnp.where(mask, value, 0.0).astype(BF16)
+            pair_row(s * BATCH + u)
+            band_row(2 * RIM + (s + 1) * BATCH + u)
         return 0
 
+    lax.fori_loop(0, 2 * RIM // BATCH + 1, first_band_rows, 0)
     lax.fori_loop(0, SLAB // BATCH, pair_rows, 0)
 
     def tap_rows(q):
@@ -279,6 +296,14 @@
         return 0
 
     lax.fori_loop(0, (ROWS + RIM) // BATCH, hidden_rows, 0)
+
+    for c in far_copies:
+        c.wait()
+    core = lax.rem(me, 2)
+    near_copies = [
+        copy(5 + BEHIND + j, ahead.at[j + 2 - 2 * core], ahead.at[j + 1], me + 1 - 2 * core, half)
+        for j in range(0, REACH, 2)
+    ]
 
     def grad_rows(s, carry):
         for u in range(BATCH):
@@ -318,16 +343,7 @@
         0, ROWS // BATCH, grad_rows, (zero, (zero,) * (TILES + 1), jnp.zeros((168, 32), F32))
     )
 
-    for d in range(1, REACH + 1):
-        piece = right_terms[d // 2]
-        rsend[d] = pltpu.roll(piece, ROWS, 1) if d % 2 else piece
-    first_copy = 5 + BEHIND + REACH
-    rights = [
-        copy(first_copy + d, rsend.at[d], rrecv.at[d], hop(me, d), half)
-        for d in range(1, REACH + 1)
-    ]
-
-    for c in spread_copies:
+    for c in near_copies:
         c.wait()
     left_low = left_grad.astype(BF16)
     left_part = dot(left_low[:, :ROWS], ahead[0])
@@ -351,11 +367,20 @@
             buf[j, 8:16, :] = turned[r : r + 8, cols(1)]
         else:
             buf[j, 8:16, :] = jnp.zeros((8, LANES), F32)
+    first_copy = 5 + BEHIND + REACH
     group_copy = first_copy + REACH
     stage = []
     for s in range(1, GROUP):
         target = lax.rem(place + s, GROUP)
         stage.append(copy(group_copy + s, buf.at[target], arecv.at[s], base + target, half))
+
+    for d in range(1, REACH + 1):
+        piece = right_terms[d // 2]
+        rsend[d] = pltpu.roll(piece, ROWS, 1) if d % 2 else piece
+    rights = [
+        copy(first_copy + d, rsend.at[d], rrecv.at[d], hop(me, d), half)
+        for d in range(1, REACH + 1)
+    ]
 
     def align_rows(s, _):
         for u in range(BATCH):
@@ -385,6 +410,23 @@
     swap_copy = group_copy + GROUP
     swap = copy(swap_copy, csend, crecv, me, other)
 
+    total = buf[place]
+    for s, c in enumerate(stage):
+        c.wait()
+        total = total + arecv[s + 1]
+    brecv[plane] = total
+
+    def plane_copy(s, index, target):
+        return pltpu.make_async_remote_copy(
+            src_ref=brecv.at[index], dst_ref=brecv.at[index],
+            send_sem=plane_send.at[s], recv_sem=plane_recv.at[index],
+            device_id={"chrom": target * GROUP + place, "chan": half}, device_id_type=MESH,
+        )
+
+    planes = [(s, lax.rem(plane + s, PLANES)) for s in range(1, PLANES)]
+    for s, p in planes:
+        plane_copy(s, plane, p).start()
+
     for c in rights:
         c.wait()
     right = right_terms[0]
@@ -394,23 +436,24 @@
     lrsend[...] = jnp.concatenate([left_low, right.astype(BF16)], axis=0)
     trade = copy(swap_copy + 1, lrsend, lrrecv, me, other)
 
-    total = buf[place]
-    for s, c in enumerate(stage):
-        c.wait()
-        total = total + arecv[s + 1]
-    brecv[plane] = total
-
-    def plane_copy(s, index, target):
+    for s, p in planes:
+        plane_copy(s, plane, p).wait_send()
+        plane_copy(s, p, p).wait_recv()
+    total = brecv[0]
+    for p in range(1, PLANES):
+        total = total + brecv[p]
+    fin[place] = total * scale
+
+    def last_copy(s, index, target):
         return pltpu.make_async_remote_copy(
-            src_ref=brecv.at[index], dst_ref=brecv.at[index],
-            send_sem=plane_send.at[s], recv_sem=plane_recv.at[index],
-            device_id={"chrom": target * GROUP + place, "chan": half}, device_id_type=MESH,
-        )
-
-    planes = [(s, lax.rem(plane + s, PLANES)) for s in range(1, PLANES)]
-    for s, p in planes:
-        plane_copy(s, plane, p).start()
-
+            src_ref=fin.at[index], dst_ref=fin.at[index],
+            send_sem=last_send.at[s], recv_sem=last_recv.at[index],
+            device_id={"chrom": base + target, "chan": half}, device_id_type=MESH,
+        )
+
+    others = [(s, lax.rem(place + s, GROUP)) for s in range(1, GROUP)]
+    for s, p in others:
+        last_copy(s, place, p).start()
     emb_copy.wait_send()
     w_copy.wait()
     trade.wait()
@@ -420,24 +463,6 @@
     swap.wait()
     contacts[...] = csend[...].astype(F32) + crecv[...].astype(F32)
 
-    for s, p in planes:
-        plane_copy(s, plane, p).wait_send()
-        plane_copy(s, p, p).wait_recv()
-    total = brecv[0]
-    for p in range(1, PLANES):
-        total = total + brecv[p]
-    fin[place] = total * scale
-
-    def last_copy(s, index, target):
-        return pltpu.make_async_remote_copy(
-            src_ref=fin.at[index], dst_ref=fin.at[index],
-            send_sem=last_send.at[s], recv_sem=last_recv.at[index],
-            device_id={"chrom": base + target, "chan": half}, device_id_type=MESH,
-        )
-
-    others = [(s, lax.rem(place + s, GROUP)) for s in range(1, GROUP)]
-    for s, p in others:
-        last_copy(s, place, p).start()
     for s, p in others:
         last_copy(s, place, p).wait_send()
         last_copy(s, p, p).wait_recv()
@@ -455,11 +480,13 @@
             jax.ShapeDtypeStruct((ROWS, 256), BF16),
             jax.ShapeDtypeStruct((GROUP, 16, LANES), F32),
         ),
-        in_specs=[m] * 3 + [v] * 6,
+        in_specs=[m] * 3 + [pl.BlockSpec(memory_space=pl.ANY)] * 6,
         out_specs=[v] * 3,
         scratch_shapes=[
             pltpu.VMEM((32, 512), BF16),
             pltpu.VMEM((32, 256), BF16),
+            pltpu.VMEM((9, 16, 16), BF16),
+            pltpu.VMEM((9, 16, 16), BF16),
             pltpu.VMEM((16, 144), BF16),
             pltpu.VMEM((16, 144), BF16),
             pltpu.VMEM((16, 24), BF16),
@@ -473,7 +500,7 @@
             pltpu.VMEM((SLAB, 16, LANES), F32),
             pltpu.VMEM((TILES, SLAB, LANES), jnp.int32),
             pltpu.VMEM((SLAB, TILES, 8, LANES), F32),
-            pltpu.VMEM((SLAB + 2 * RIM, 16, OFF), F32),
+            pltpu.VMEM((SLAB + 2 * RIM + BATCH, 16, OFF), F32),
             pltpu.VMEM((5, SLAB, 16, OFF), BF16),
             pltpu.VMEM((5, SLAB, 16, OFF), BF16),
             pltpu.VMEM((SLAB, 16, OFF), BF16),
@@ -489,6 +516,7 @@
             pltpu.VMEM((GROUP, 16, LANES), F32),
             pltpu.VMEM((GROUP, 16, LANES), F32),
             pltpu.VMEM((PLANES, 16, LANES), F32),
+            dma((6,)),
             dma((copies,)),
             dma((copies,)),
             dma((PLANES,)),

time: 67.1 us -> 60.7 us (0.905)
  Pallas kernels: 66.3 us -> 60 us
    pallas_call x1, Pallas kernels: 64.3 us -> 58.1 us  [band_call(): pl.pallas_call(functools.partial(band_kernel, scale), out_shape=(jax.Shap...]
where the time goes in v4:
time: 60.7 us; the launch traced here: 60.6 us
  Pallas kernels  60 us (99%)
  between operations  0.64 us (1%)
    pallas_call x1, Pallas kernels, band_call(): pl.pallas_call(functools.partial(band_kernel, scale), out_shape=(jax.Shap...  58.1 us
    pallas_call x1, Pallas kernels, output_call(): pl.pallas_call(output_kernel, out_shape=(jax.ShapeDtypeStruct((ROWS, OFF)...  1.92 us

profile of v4, /device:TPU:1, one launch (start us, length us, event | category | flops | bytes accessed | tf_op | source)
XLA Modules:
  0.0 60.6 jit_solution(16116919467990728273)
XLA Ops:
  0.6 58.1 %shard_map.144 = (f32[64,512]{1,0:T(8,128)}, bf16[64,256]{1,0:T(8,128)(2,1)}, f32[16,16,128]{2,1,0:T(8,128)}) custom-call(s32[8]{0:T(128)} %ends.1, s32[2]{0:T(128)} %dil.1, f32[16]{0:T(128)} %head.3, bf16[64,256]{1,0:T(8,128)(2,1)} %emb.1, bf16[16,512]{1,0:T(8,128)(2,1)} %bitcast.20, bf16[16,512]{1,0:T(8,128)(2,1)} %bitcast.21, ...), custom_call_target="tpu_custom_call" | custom-call | tf_op jit(solution)/shard_map/pallas_call | solution.py:476
  58.7 1.9 %shard_map.145 = (f32[64,512]{1,0:T(8,128)}, bf16[64,256]{1,0:T(8,128)(2,1)}, f32[16,512]{1,0:T(8,128)}, f32[16,512]{1,0:T(8,128)}, f32[9,16,16]{2,1,0:T(8,128)}, /*index=5*/f32[9,16,16]{2,1,0:T(8,128)}, f32[1,16]{1,0:T(1,128)}) custom-call(f32[16]{0:T(128)} %head.3, f32[16,16,128]{2,1,0:T(8,128)} %get-tuple-element.17.fin, bf16[9,16,16]{2,1,0:T(8,128)(2,1)} %bitcast.18, ...), custom_call_target="tpu_custom_call" | custom-call | tf_op jit(solution)/shard_map/pallas_call | solution.py:567

commit v5 on v4

--- a/solution.py
+++ b/solution.py
@@ -21,6 +21,7 @@
 BEHIND = REACH + 1
 TAPS = (-1, 0, 1)
 BATCH = 8
+WIDE = 1
 GROUP = 16
 PLANES = 8
 INV_ROOT_TWO = 0.7071067811865476
@@ -80,7 +81,7 @@
     ends, dil, head, emb, w_left, w_right, first_in, second_in, cot,
     contacts, emb_grad, fin,
     wt, wother, first_w, second_w, w1, w1t, vm, zw,
-    full, ahead, slots, cot96, rb, lb, lcol, edge, vga, band, px, gy, hid, z, zs, acc,
+    full, slots, cot96, rb, lb, lcol, edge, vga, band, px, gy, hid, z, zs, acc,
     csend, crecv, rsend, rrecv, lrsend, lrrecv, buf, arecv, brecv,
     load_sem, send_sem, recv_sem, plane_send, plane_recv, last_send, last_recv,
 ):
@@ -172,12 +173,6 @@
         for d in range(1, BEHIND + 1)
     ]
     tiles.append(copy(4 + BEHIND, slots.at[1], slots.at[0], hop(me, 1), half))
-    ahead[0] = full[...]
-    far_copies = [
-        copy(4 + BEHIND + d, full, ahead.at[d], hop(me, -d), half)
-        for d in range(2, REACH + 1, 2)
-    ]
-
     for c in rims:
         c.wait()
     big = jnp.int32(1 << 30)
@@ -297,14 +292,6 @@
 
     lax.fori_loop(0, (ROWS + RIM) // BATCH, hidden_rows, 0)
 
-    for c in far_copies:
-        c.wait()
-    core = lax.rem(me, 2)
-    near_copies = [
-        copy(5 + BEHIND + j, ahead.at[j + 2 - 2 * core], ahead.at[j + 1], me + 1 - 2 * core, half)
-        for j in range(0, REACH, 2)
-    ]
-
     def grad_rows(s, carry):
         for u in range(BATCH):
             carry = grad_row(s * BATCH + u, carry)
@@ -313,7 +300,7 @@
     head_full = head_column(head, LANES)
 
     def grad_row(row, carry):
-        left_acc, right_acc, weight_acc = carry
+        left_acc, right_acc = carry
         q = row + RIM
         stack = jnp.concatenate([gy[b - a + 2, q - a * d1] for a in TAPS for b in TAPS], axis=0)
         grad_pair = dot(w1t[...], stack)
@@ -331,56 +318,40 @@
             r + jnp.where(lane < row, b, a)
             for r, b, a in zip(right_acc, [zero] + spread, spread + [zero])
         )
-        weight_acc = weight_acc + dot(
-            jnp.concatenate([stack, tap_rows(q)], axis=0),
-            jnp.concatenate([px[2, q], hid[q]], axis=0),
-            LAST,
-        )
-        return left_acc, right_acc, weight_acc
+        return left_acc, right_acc
 
     zero = jnp.zeros((16, LANES), F32)
-    left_grad, right_terms, weight_acc = lax.fori_loop(
-        0, ROWS // BATCH, grad_rows, (zero, (zero,) * (TILES + 1), jnp.zeros((168, 32), F32))
-    )
-
-    for c in near_copies:
-        c.wait()
-    left_low = left_grad.astype(BF16)
-    left_part = dot(left_low[:, :ROWS], ahead[0])
-    right_part = jnp.zeros((16, OFF), F32)
-    for t in range(TILES):
-        pair_of = jnp.concatenate([ahead[2 * t], ahead[2 * t + 1]], axis=0)
-        right_part = right_part + dot(right_terms[t].astype(BF16), pair_of)
-    right_part = right_part + dot(right_terms[TILES][:, :ROWS].astype(BF16), ahead[REACH])
-    acc[...] = jnp.zeros((256, LANES), F32)
-    acc[:168, :32] = weight_acc
-    turned = acc[...].T
-    for j in range(GROUP):
-        part = left_part if j < 8 else right_part
-        r = 8 * ((j // 4) % 2)
-        buf[j, 0:8, :] = part[r : r + 8, cols(j % 4)]
-        if j < 4:
-            r = 8 * (j // 2)
-            buf[j, 8:16, :] = turned[r : r + 8, cols(j % 2)]
-        elif j < 6:
-            r = 8 * (j - 2)
-            buf[j, 8:16, :] = turned[r : r + 8, cols(1)]
-        else:
-            buf[j, 8:16, :] = jnp.zeros((8, LANES), F32)
-    first_copy = 5 + BEHIND + REACH
-    group_copy = first_copy + REACH
-    stage = []
-    for s in range(1, GROUP):
-        target = lax.rem(place + s, GROUP)
-        stage.append(copy(group_copy + s, buf.at[target], arecv.at[s], base + target, half))
+    left_grad, right_terms = lax.fori_loop(
+        0, ROWS // BATCH, grad_rows, (zero, (zero,) * (TILES + 1))
+    )
 
     for d in range(1, REACH + 1):
         piece = right_terms[d // 2]
         rsend[d] = pltpu.roll(piece, ROWS, 1) if d % 2 else piece
+    first_copy = 5 + BEHIND
     rights = [
         copy(first_copy + d, rsend.at[d], rrecv.at[d], hop(me, d), half)
         for d in range(1, REACH + 1)
     ]
+
+    def weight_rows(s, weight_acc):
+        for u in range(0, BATCH, WIDE):
+            left_side, right_side = [], []
+            for n in range(WIDE):
+                q = RIM + s * BATCH + u + n
+                taken = [gy[b - a + 2, q - a * d1] for a in TAPS for b in TAPS]
+                left_side.append(jnp.concatenate(taken + [tap_rows(q)], axis=0))
+                right_side.append(jnp.concatenate([px[2, q], hid[q]], axis=0))
+            weight_acc = weight_acc + dot(
+                jnp.concatenate(left_side, axis=1), jnp.concatenate(right_side, axis=1), LAST
+            )
+        return weight_acc
+
+    acc[...] = jnp.zeros((256, LANES), F32)
+    acc[:168, :32] = lax.fori_loop(
+        0, ROWS // BATCH, weight_rows, jnp.zeros((168, 32), F32)
+    )
+    turned = acc[...].T
 
     def align_rows(s, _):
         for u in range(BATCH):
@@ -407,8 +378,35 @@
     for t in range(TILES):
         second = jnp.where(own_lane < edge[t, RIM : RIM + ROWS, :], total[t], 0.0)
         csend[:, cols(t)] = (tap_sum(t, 0, 9) + second).astype(BF16)
-    swap_copy = group_copy + GROUP
+    swap_copy = first_copy + REACH + 1
     swap = copy(swap_copy, csend, crecv, me, other)
+
+    for c in rights:
+        c.wait()
+    right = right_terms[0]
+    for d in range(1, REACH + 1):
+        right = right + rrecv[d]
+    right = jnp.where(lane < ROWS, right, 0.0)
+    lrsend[...] = jnp.concatenate([left_grad, right], axis=0).astype(BF16)
+    trade = copy(swap_copy + 1, lrsend, lrrecv, me, other)
+
+    part = dot(lrsend[:, :ROWS], full[...])
+    for j in range(GROUP):
+        r = 8 * (j // 4)
+        buf[j, 0:8, :] = part[r : r + 8, cols(j % 4)]
+        if j < 4:
+            r = 8 * (j // 2)
+            buf[j, 8:16, :] = turned[r : r + 8, cols(j % 2)]
+        elif j < 6:
+            r = 8 * (j - 2)
+            buf[j, 8:16, :] = turned[r : r + 8, cols(1)]
+        else:
+            buf[j, 8:16, :] = jnp.zeros((8, LANES), F32)
+    group_copy = swap_copy + 1
+    stage = []
+    for s in range(1, GROUP):
+        target = lax.rem(place + s, GROUP)
+        stage.append(copy(group_copy + s, buf.at[target], arecv.at[s], base + target, half))
 
     total = buf[place]
     for s, c in enumerate(stage):
@@ -426,15 +424,6 @@
     planes = [(s, lax.rem(plane + s, PLANES)) for s in range(1, PLANES)]
     for s, p in planes:
         plane_copy(s, plane, p).start()
-
-    for c in rights:
-        c.wait()
-    right = right_terms[0]
-    for d in range(1, REACH + 1):
-        right = right + rrecv[d]
-    right = jnp.where(lane < ROWS, right, 0.0)
-    lrsend[...] = jnp.concatenate([left_low, right.astype(BF16)], axis=0)
-    trade = copy(swap_copy + 1, lrsend, lrrecv, me, other)
 
     for s, p in planes:
         plane_copy(s, plane, p).wait_send()
@@ -471,7 +460,7 @@
 def band_call(scale, *operands):
     v = pl.BlockSpec(memory_space=pltpu.VMEM)
     m = pl.BlockSpec(memory_space=pltpu.SMEM)
-    copies = 4 + BEHIND + REACH + 1 + REACH + GROUP + 4
+    copies = 5 + BEHIND + REACH + 3 + GROUP
     dma = pltpu.SemaphoreType.DMA
     return pl.pallas_call(
         functools.partial(band_kernel, scale),
@@ -492,7 +481,6 @@
             pltpu.VMEM((16, 24), BF16),
             pltpu.VMEM((16, 32), BF16),
             pltpu.VMEM((ROWS, 512), BF16),
-            pltpu.VMEM((REACH + 1, ROWS, 512), BF16),
             pltpu.VMEM((BEHIND + 2, 16, LANES), F32),
             pltpu.VMEM((SLAB, OFF), BF16),
             pltpu.VMEM((16, OFF + LANES), F32),

time: 60.7 us -> 57.6 us (0.949)
  Pallas kernels: 60 us -> 56.8 us
    pallas_call x1, Pallas kernels: 58.1 us -> 54.9 us  [band_call(): pl.pallas_call(functools.partial(band_kernel, scale), out_shape=(jax.Shap...]
where the time goes in v5:
time: 57.6 us; the launch traced here: 57.4 us
  Pallas kernels  56.8 us (99%)
  between operations  0.64 us (1%)
    pallas_call x1, Pallas kernels, band_call(): pl.pallas_call(functools.partial(band_kernel, scale), out_shape=(jax.Shap...  54.9 us
    pallas_call x1, Pallas kernels, output_call(): pl.pallas_call(output_kernel, out_shape=(jax.ShapeDtypeStruct((ROWS, OFF)...  1.92 us

profile of v5, /device:TPU:1, one launch (start us, length us, event | category | flops | bytes accessed | tf_op | source)
XLA Modules:
  0.0 57.4 jit_solution(2457946128771845867)
XLA Ops:
  0.6 54.9 %shard_map.144 = (f32[64,512]{1,0:T(8,128)}, bf16[64,256]{1,0:T(8,128)(2,1)}, f32[16,16,128]{2,1,0:T(8,128)}) custom-call(s32[8]{0:T(128)} %ends.1, s32[2]{0:T(128)} %dil.1, f32[16]{0:T(128)} %head.3, bf16[64,256]{1,0:T(8,128)(2,1)} %emb.1, bf16[16,512]{1,0:T(8,128)(2,1)} %bitcast.20, bf16[16,512]{1,0:T(8,128)(2,1)} %bitcast.21, ...), custom_call_target="tpu_custom_call" | custom-call | tf_op jit(solution)/shard_map/pallas_call | solution.py:465
  55.5 1.9 %shard_map.145 = (f32[64,512]{1,0:T(8,128)}, bf16[64,256]{1,0:T(8,128)(2,1)}, f32[16,512]{1,0:T(8,128)}, f32[16,512]{1,0:T(8,128)}, f32[9,16,16]{2,1,0:T(8,128)}, /*index=5*/f32[9,16,16]{2,1,0:T(8,128)}, f32[1,16]{1,0:T(1,128)}) custom-call(f32[16]{0:T(128)} %head.3, f32[16,16,128]{2,1,0:T(8,128)} %get-tuple-element.17.fin, bf16[9,16,16]{2,1,0:T(8,128)(2,1)} %bitcast.18, ...), custom_call_target="tpu_custom_call" | custom-call | tf_op jit(solution)/shard_map/pallas_call | solution.py:555

commit v6 on v5

--- a/solution.py
+++ b/solution.py
@@ -21,11 +21,12 @@
 BEHIND = REACH + 1
 TAPS = (-1, 0, 1)
 BATCH = 8
-WIDE = 1
+WIDE = 16
 GROUP = 16
 PLANES = 8
 INV_ROOT_TWO = 0.7071067811865476
-INV_ROOT_TWO_PI = 0.3989422804014327
+TWO_OVER_ROOT_PI = 1.1283791670955126
+LOG2_E = 1.4426950408889634
 LAST = (((1,), (1,)), ((), ()))
 FIRST = (((0,), (0,)), ((), ()))
 
@@ -71,15 +72,16 @@
 def head_column(head, lanes):
     sub = ids((16, lanes), 0)
     column = jnp.zeros((16, lanes), F32)
-    for o in range(16):
+    for o in range(WIDE):
         column = jnp.where(sub == o, head[o], column)
     return column
 
 
 def band_kernel(
     scale,
-    ends, dil, head, emb, w_left, w_right, first_in, second_in, cot,
+    ends_in, dil_in, head_in, emb, w_left, w_right, first_in, second_in, cot,
     contacts, emb_grad, fin,
+    ends, dil, head,
     wt, wother, first_w, second_w, w1, w1t, vm, zw,
     full, slots, cot96, rb, lb, lcol, edge, vga, band, px, gy, hid, z, zs, acc,
     csend, crecv, rsend, rrecv, lrsend, lrrecv, buf, arecv, brecv,
@@ -93,8 +95,6 @@
     base = me - place
     mine = pl.ds(pl.multiple_of(half * 256, 256), 256)
     theirs = pl.ds(pl.multiple_of(other * 256, 256), 256)
-    d1 = dil[0]
-    d2 = dil[1]
     lane = ids((16, LANES), 1)
 
     barrier = pltpu.get_barrier_semaphore()
@@ -126,6 +126,9 @@
                 (first_in, first_w),
                 (second_in, second_w),
                 (cot, cot96.at[pl.ds(RIM, ROWS)]),
+                (ends_in, ends),
+                (dil_in, dil),
+                (head_in, head),
             ]
         )
     ]
@@ -140,6 +143,8 @@
     ]
     for load in loads:
         load.wait()
+    d1 = dil[0]
+    d2 = dil[1]
     w_copy = copy(3, wt.at[:, theirs], wother, me, other)
 
     head16 = head_column(head, 16)
@@ -159,11 +164,12 @@
     rows = rows.astype(BF16)
     low = (ids((16, 32), 1) == ids((16, 32), 0)).astype(BF16)
     high = (ids((16, 32), 1) == ids((16, 32), 0) + 16).astype(BF16)
-    zw[...] = (dot(rows, low) + dot(head_rows, high)).astype(BF16)
+    half_rows = rows * jnp.bfloat16(0.5)
+    zw[...] = (dot(half_rows, low) + dot(head_rows, high)).astype(BF16)
     tap = ids((16, 24), 0)
     column = tap + 4 * ((tap >= 3).astype(jnp.int32) + (tap >= 6).astype(jnp.int32)) + 2
     spot = ((ids((16, 24), 1) == column) & (tap < 9)).astype(BF16)
-    vm[...] = dot(rows, spot, FIRST).astype(BF16)
+    vm[...] = dot(half_rows, spot, FIRST).astype(BF16)
 
     emb_copy.wait_recv()
     twice = jnp.concatenate([full[...], full[...]], axis=0)
@@ -261,8 +267,9 @@
     def hidden_values(q, first, grad_hidden):
         mask = jnp.concatenate(masks(q), axis=1)
         first = jnp.where(mask, first, 0.0)
-        cdf = 0.5 * (1.0 + lax.erf(first * INV_ROOT_TWO))
-        slope = cdf + first * jnp.exp(-0.5 * first * first) * INV_ROOT_TWO_PI
+        scaled = first * INV_ROOT_TWO
+        cdf = 1.0 + lax.erf(scaled)
+        slope = cdf + scaled * jnp.exp2(scaled * scaled * -LOG2_E) * TWO_OVER_ROOT_PI
         hidden = (first * cdf).astype(BF16)
         grad_first = jnp.where(mask, slope * grad_hidden, 0.0).astype(BF16)
         parts = [grad_first[:, cols(t)] for t in range(TILES)]
@@ -270,31 +277,23 @@
             for t, tile in enumerate(shift_tiles(parts, e, d1)):
                 gy[e + 2, q, :, cols(t)] = tile
         hid[q] = hidden
-        return hidden
-
-    def head_dot(q, hidden):
-        out = dot(zw[...], jnp.concatenate([hidden, px[2, q]], axis=0))
-        for t in range(TILES):
-            z[q, t] = out[:, cols(t)]
 
     def hidden_rows(s, _):
-        lag, more = 3, 2
-        dots, values = {}, {}
-        for u in range(BATCH + lag + more):
-            q = RIM // 2 + s * BATCH + u
-            if u < BATCH:
+        lag = 3
+        dots = {}
+        for u in range(WIDE + lag):
+            q = RIM // 2 + s * WIDE + u
+            if u < WIDE:
                 dots[u] = hidden_dots(q)
-            if 0 <= u - lag < BATCH:
-                values[u - lag] = hidden_values(q - lag, *dots.pop(u - lag))
-            if u >= lag + more:
-                head_dot(q - lag - more, values.pop(u - lag - more))
+            if u >= lag:
+                hidden_values(q - lag, *dots.pop(u - lag))
         return 0
 
-    lax.fori_loop(0, (ROWS + RIM) // BATCH, hidden_rows, 0)
+    lax.fori_loop(0, (ROWS + RIM) // WIDE, hidden_rows, 0)
 
     def grad_rows(s, carry):
-        for u in range(BATCH):
-            carry = grad_row(s * BATCH + u, carry)
+        for u in range(WIDE):
+            carry = grad_row(s * WIDE + u, carry)
         return carry
 
     head_full = head_column(head, LANES)
@@ -322,7 +321,7 @@
 
     zero = jnp.zeros((16, LANES), F32)
     left_grad, right_terms = lax.fori_loop(
-        0, ROWS // BATCH, grad_rows, (zero, (zero,) * (TILES + 1))
+        0, ROWS // WIDE, grad_rows, (zero, (zero,) * (TILES + 1))
     )
 
     for d in range(1, REACH + 1):
@@ -335,52 +334,23 @@
     ]
 
     def weight_rows(s, weight_acc):
-        for u in range(0, BATCH, WIDE):
-            left_side, right_side = [], []
-            for n in range(WIDE):
-                q = RIM + s * BATCH + u + n
-                taken = [gy[b - a + 2, q - a * d1] for a in TAPS for b in TAPS]
-                left_side.append(jnp.concatenate(taken + [tap_rows(q)], axis=0))
-                right_side.append(jnp.concatenate([px[2, q], hid[q]], axis=0))
+        for u in range(WIDE):
+            q = RIM + s * WIDE + u
+            taken = [gy[b - a + 2, q - a * d1] for a in TAPS for b in TAPS]
             weight_acc = weight_acc + dot(
-                jnp.concatenate(left_side, axis=1), jnp.concatenate(right_side, axis=1), LAST
+                jnp.concatenate(taken + [tap_rows(q)], axis=0),
+                jnp.concatenate([px[2, q], hid[q]], axis=0),
+                LAST,
             )
         return weight_acc
 
     acc[...] = jnp.zeros((256, LANES), F32)
     acc[:168, :32] = lax.fori_loop(
-        0, ROWS // BATCH, weight_rows, jnp.zeros((168, 32), F32)
+        0, ROWS // WIDE, weight_rows, jnp.zeros((168, 32), F32)
     )
     turned = acc[...].T
 
-    def align_rows(s, _):
-        for u in range(BATCH):
-            row = s * BATCH + u
-            for n, a in enumerate(TAPS):
-                for t in range(TILES):
-                    zs[n, t, pl.ds(pl.multiple_of(row * 16, 16), 16), :] = z[row + RIM + a * d2, t]
-        return 0
-
-    lax.fori_loop(0, ROWS // BATCH, align_rows, 0)
-
-    def tap_sum(t, a, row):
-        return zs[a + 1, t, pl.ds(row, ROWS, stride=16), :]
-
-    total = None
-    for e in range(-2, 3):
-        parts = [
-            sum(tap_sum(t, a, (a + 1) * 3 + a + e + 1) for a in TAPS if -1 <= a + e <= 1)
-            for t in range(TILES)
-        ]
-        parts = shift_tiles(parts, -e, d2)
-        total = parts if total is None else [x + y for x, y in zip(total, parts)]
-    own_lane = ids((ROWS, LANES), 1)
-    for t in range(TILES):
-        second = jnp.where(own_lane < edge[t, RIM : RIM + ROWS, :], total[t], 0.0)
-        csend[:, cols(t)] = (tap_sum(t, 0, 9) + second).astype(BF16)
     swap_copy = first_copy + REACH + 1
-    swap = copy(swap_copy, csend, crecv, me, other)
-
     for c in rights:
         c.wait()
     right = right_terms[0]
@@ -408,6 +378,43 @@
         target = lax.rem(place + s, GROUP)
         stage.append(copy(group_copy + s, buf.at[target], arecv.at[s], base + target, half))
 
+    def head_rows_of(s, _):
+        for u in range(BATCH):
+            q = RIM // 2 + s * BATCH + u
+            out = dot(zw[...], jnp.concatenate([hid[q], px[2, q]], axis=0))
+            for t in range(TILES):
+                z[q, t] = out[:, cols(t)]
+        return 0
+
+    lax.fori_loop(0, (ROWS + RIM) // BATCH, head_rows_of, 0)
+
+    def align_rows(s, _):
+        for u in range(BATCH):
+            row = s * BATCH + u
+            for n, a in enumerate(TAPS):
+                for t in range(TILES):
+                    zs[n, t, pl.ds(pl.multiple_of(row * 16, 16), 16), :] = z[row + RIM + a * d2, t]
+        return 0
+
+    lax.fori_loop(0, ROWS // BATCH, align_rows, 0)
+
+    def tap_sum(t, a, row):
+        return zs[a + 1, t, pl.ds(row, ROWS, stride=16), :]
+
+    total = None
+    for e in range(-2, 3):
+        parts = [
+            sum(tap_sum(t, a, (a + 1) * 3 + a + e + 1) for a in TAPS if -1 <= a + e <= 1)
+            for t in range(TILES)
+        ]
+        parts = shift_tiles(parts, -e, d2)
+        total = parts if total is None else [x + y for x, y in zip(total, parts)]
+    own_lane = ids((ROWS, LANES), 1)
+    for t in range(TILES):
+        second = jnp.where(own_lane < edge[t, RIM : RIM + ROWS, :], total[t], 0.0)
+        csend[:, cols(t)] = (tap_sum(t, 0, 9) + second).astype(BF16)
+    swap = copy(swap_copy, csend, crecv, me, other)
+
     total = buf[place]
     for s, c in enumerate(stage):
         c.wait()
@@ -459,7 +466,6 @@
 
 def band_call(scale, *operands):
     v = pl.BlockSpec(memory_space=pltpu.VMEM)
-    m = pl.BlockSpec(memory_space=pltpu.SMEM)
     copies = 5 + BEHIND + REACH + 3 + GROUP
     dma = pltpu.SemaphoreType.DMA
     return pl.pallas_call(
@@ -469,9 +475,12 @@
             jax.ShapeDtypeStruct((ROWS, 256), BF16),
             jax.ShapeDtypeStruct((GROUP, 16, LANES), F32),
         ),
-        in_specs=[m] * 3 + [pl.BlockSpec(memory_space=pl.ANY)] * 6,
+        in_specs=[pl.BlockSpec(memory_space=pltpu.HBM)] * 9,
         out_specs=[v] * 3,
         scratch_shapes=[
+            pltpu.SMEM((8,), jnp.int32),
+            pltpu.SMEM((2,), jnp.int32),
+            pltpu.SMEM((16,), F32),
             pltpu.VMEM((32, 512), BF16),
             pltpu.VMEM((32, 256), BF16),
             pltpu.VMEM((9, 16, 16), BF16),
@@ -504,7 +513,7 @@
             pltpu.VMEM((GROUP, 16, LANES), F32),
             pltpu.VMEM((GROUP, 16, LANES), F32),
             pltpu.VMEM((PLANES, 16, LANES), F32),
-            dma((6,)),
+            dma((9,)),
             dma((copies,)),
             dma((copies,)),
             dma((PLANES,)),
@@ -542,7 +551,7 @@
         a, b = ab // 3, ab % 3
         first_grad[ab] = turned[16 * ab : 16 * ab + 16, :16]
         row = 2 * LANES + 16 + 8 * a + (b - a + 2)
-        moved = turned[row : row + 1, :16]
+        moved = 0.5 * turned[row : row + 1, :16]
         second_grad[ab] = head16 * moved
         sums = sums + second_w[ab].astype(F32) * moved
     total = head_sum + jnp.sum(sums, axis=1, keepdims=True)

time: 57.6 us -> 54.2 us (0.941)
  Pallas kernels: 56.8 us -> 53.5 us
    pallas_call x1, Pallas kernels: 54.9 us -> 51.5 us  [band_call(): pl.pallas_call(functools.partial(band_kernel, scale), out_shape=(jax.Shap...]
where the time goes in v6:
time: 54.2 us; the launch traced here: 54.1 us
  Pallas kernels  53.5 us (99%)
  between operations  0.64 us (1%)
    pallas_call x1, Pallas kernels, band_call(): pl.pallas_call(functools.partial(band_kernel, scale), out_shape=(jax.Shap...  51.5 us
    pallas_call x1, Pallas kernels, output_call(): pl.pallas_call(output_kernel, out_shape=(jax.ShapeDtypeStruct((ROWS, OFF)...  1.94 us

profile of v6, /device:TPU:1, one launch (start us, length us, event | category | flops | bytes accessed | tf_op | source)
XLA Modules:
  0.0 54.1 jit_solution(16019262947947841911)
XLA Ops:
  0.6 51.5 %shard_map.144 = (f32[64,512]{1,0:T(8,128)}, bf16[64,256]{1,0:T(8,128)(2,1)}, f32[16,16,128]{2,1,0:T(8,128)}) custom-call(s32[8]{0:T(128)} %ends_in.1, s32[2]{0:T(128)} %dil_in.1, f32[16]{0:T(128)} %head.1, bf16[64,256]{1,0:T(8,128)(2,1)} %emb.1, bf16[16,512]{1,0:T(8,128)(2,1)} %bitcast.20, bf16[16,512]{1,0:T(8,128)(2,1)} %bitcast.21, ...), custom_call_target="tpu_custom_call" | custom-call | tf_op jit(solution)/shard_map/pallas_call | solution.py:471
  52.2 1.9 %shard_map.145 = (f32[64,512]{1,0:T(8,128)}, bf16[64,256]{1,0:T(8,128)(2,1)}, f32[16,512]{1,0:T(8,128)}, f32[16,512]{1,0:T(8,128)}, f32[9,16,16]{2,1,0:T(8,128)}, /*index=5*/f32[9,16,16]{2,1,0:T(8,128)}, f32[1,16]{1,0:T(1,128)}) custom-call(f32[16]{0:T(128)} %head.1, f32[16,16,128]{2,1,0:T(8,128)} %get-tuple-element.17.fin, bf16[9,16,16]{2,1,0:T(8,128)(2,1)} %bitcast.18, ...), custom_call_target="tpu_custom_call" | custom-call | tf_op jit(solution)/shard_map/pallas_call | solution.py:564

commit v7 on v6

--- a/solution.py
+++ b/solution.py
@@ -22,6 +22,7 @@
 TAPS = (-1, 0, 1)
 BATCH = 8
 WIDE = 16
+LONG = 40
 GROUP = 16
 PLANES = 8
 INV_ROOT_TWO = 0.7071067811865476
@@ -83,7 +84,7 @@
     contacts, emb_grad, fin,
     ends, dil, head,
     wt, wother, first_w, second_w, w1, w1t, vm, zw,
-    full, slots, cot96, rb, lb, lcol, edge, vga, band, px, gy, hid, z, zs, acc,
+    full, slots, cot96, rb, lb, lcol, edge, vga, band, px, gy, hid, parts_of, z, zs, acc,
     csend, crecv, rsend, rrecv, lrsend, lrrecv, buf, arecv, brecv,
     load_sem, send_sem, recv_sem, plane_send, plane_recv, last_send, last_recv,
 ):
@@ -201,20 +202,22 @@
         for t in range(TILES):
             vga[:, t, e, :] = jnp.zeros((SLAB, LANES), F32)
 
-    for c in tiles:
+    for c in (tiles[-1], tiles[0]):
         c.wait()
+    lb[...] = jnp.where(
+        lane < RIM,
+        pltpu.roll(slots[0], 16, 1),
+        jnp.where(lane < RIM + ROWS, pltpu.roll(slots[1], 80, 1), pltpu.roll(slots[2], 16, 1)),
+    )
+    for q in range(SLAB):
+        lcol[q] = jnp.broadcast_to(lb[:, q : q + 1], (16, LANES))
     for t in range(TILES + 1):
+        for c in tiles[max(2 * t - 1, 1) : min(2 * t + 1, BEHIND)]:
+            c.wait()
         before = pltpu.roll(slots[2 * t], 96, 1)
         inside = pltpu.roll(slots[2 * t + 1], 32, 1)
         after = pltpu.roll(slots[2 * t + 2], 96, 1)
         rb[:, cols(t)] = jnp.where(lane < 32, before, jnp.where(lane < 96, inside, after))
-    lb[...] = jnp.where(
-        lane < RIM,
-        pltpu.roll(slots[0], 16, 1),
-        jnp.where(lane < RIM + ROWS, pltpu.roll(slots[1], 80, 1), pltpu.roll(slots[2], 16, 1)),
-    )
-    for q in range(SLAB):
-        lcol[q] = jnp.broadcast_to(lb[:, q : q + 1], (16, LANES))
 
     def masks(q):
         return [lane < edge[t, pl.ds(q, 1), :] for t in range(TILES)]
@@ -281,15 +284,15 @@
     def hidden_rows(s, _):
         lag = 3
         dots = {}
-        for u in range(WIDE + lag):
-            q = RIM // 2 + s * WIDE + u
-            if u < WIDE:
+        for u in range(LONG + lag):
+            q = RIM // 2 + s * LONG + u
+            if u < LONG:
                 dots[u] = hidden_dots(q)
             if u >= lag:
                 hidden_values(q - lag, *dots.pop(u - lag))
         return 0
 
-    lax.fori_loop(0, (ROWS + RIM) // WIDE, hidden_rows, 0)
+    lax.fori_loop(0, (ROWS + RIM) // LONG, hidden_rows, 0)
 
     def grad_rows(s, carry):
         for u in range(WIDE):
@@ -298,30 +301,25 @@
 
     head_full = head_column(head, LANES)
 
-    def grad_row(row, carry):
-        left_acc, right_acc = carry
+    def grad_row(row, right_acc):
         q = row + RIM
         stack = jnp.concatenate([gy[b - a + 2, q - a * d1] for a in TAPS for b in TAPS], axis=0)
         grad_pair = dot(w1t[...], stack)
         left = lcol[q]
-        prods, spread = [], []
+        spread = []
         for t, mask in enumerate(masks(q)):
             g = vga[q, t, 2:3, :]
             part = jnp.where(mask, grad_pair[:, cols(t)] + head_full * g, 0.0)
-            prods.append(part * band[q + RIM, :, cols(t)])
+            parts_of[row, :, cols(t)] = part
             spread.append(pltpu.roll(part * left, row, 1))
-        total = (prods[0] + prods[1]) + (prods[2] + prods[3])
-        left_acc = jnp.where(lane == row, jnp.sum(total, axis=1, keepdims=True), left_acc)
         zero = jnp.zeros((16, LANES), F32)
-        right_acc = tuple(
+        return tuple(
             r + jnp.where(lane < row, b, a)
             for r, b, a in zip(right_acc, [zero] + spread, spread + [zero])
         )
-        return left_acc, right_acc
-
-    zero = jnp.zeros((16, LANES), F32)
-    left_grad, right_terms = lax.fori_loop(
-        0, ROWS // WIDE, grad_rows, (zero, (zero,) * (TILES + 1))
+
+    right_terms = lax.fori_loop(
+        0, ROWS // WIDE, grad_rows, (jnp.zeros((16, LANES), F32),) * (TILES + 1)
     )
 
     for d in range(1, REACH + 1):
@@ -332,6 +330,18 @@
         copy(first_copy + d, rsend.at[d], rrecv.at[d], hop(me, d), half)
         for d in range(1, REACH + 1)
     ]
+
+    def left_rows(s, left_acc):
+        for u in range(WIDE):
+            row = s * WIDE + u
+            prods = [
+                parts_of[row, :, cols(t)] * band[row + 2 * RIM, :, cols(t)] for t in range(TILES)
+            ]
+            total = (prods[0] + prods[1]) + (prods[2] + prods[3])
+            left_acc = jnp.where(lane == row, jnp.sum(total, axis=1, keepdims=True), left_acc)
+        return left_acc
+
+    left_grad = lax.fori_loop(0, ROWS // WIDE, left_rows, jnp.zeros((16, LANES), F32))
 
     def weight_rows(s, weight_acc):
         for u in range(WIDE):
@@ -501,6 +511,7 @@
             pltpu.VMEM((5, SLAB, 16, OFF), BF16),
             pltpu.VMEM((5, SLAB, 16, OFF), BF16),
             pltpu.VMEM((SLAB, 16, OFF), BF16),
+            pltpu.VMEM((ROWS, 16, OFF), F32),
             pltpu.VMEM((SLAB, TILES, 16, LANES), F32),
             pltpu.VMEM((3, TILES, ROWS * 16, LANES), F32),
             pltpu.VMEM((256, LANES), F32),

time: 54.2 us -> 52.7 us (0.972)
  Pallas kernels: 53.5 us -> 52 us
    pallas_call x1, Pallas kernels: 51.5 us -> 50 us  [band_call(): pl.pallas_call(functools.partial(band_kernel, scale), out_shape=(jax.Shap...]
where the time goes in v7:
time: 52.7 us; the launch traced here: 52.6 us
  Pallas kernels  52 us (99%)
  between operations  0.64 us (1%)
    pallas_call x1, Pallas kernels, band_call(): pl.pallas_call(functools.partial(band_kernel, scale), out_shape=(jax.Shap...  50 us
    pallas_call x1, Pallas kernels, output_call(): pl.pallas_call(output_kernel, out_shape=(jax.ShapeDtypeStruct((ROWS, OFF)...  1.94 us

profile of v7, /device:TPU:1, one launch (start us, length us, event | category | flops | bytes accessed | tf_op | source)
XLA Modules:
  0.0 52.6 jit_solution(3941111562237705173)
XLA Ops:
  0.6 50.0 %shard_map.144 = (f32[64,512]{1,0:T(8,128)}, bf16[64,256]{1,0:T(8,128)(2,1)}, f32[16,16,128]{2,1,0:T(8,128)}) custom-call(s32[8]{0:T(128)} %ends_in.1, s32[2]{0:T(128)} %dil_in.1, f32[16]{0:T(128)} %head.1, bf16[64,256]{1,0:T(8,128)(2,1)} %emb.1, bf16[16,512]{1,0:T(8,128)(2,1)} %bitcast.20, bf16[16,512]{1,0:T(8,128)(2,1)} %bitcast.21, ...), custom_call_target="tpu_custom_call" | custom-call | tf_op jit(solution)/shard_map/pallas_call | solution.py:481
  50.7 1.9 %shard_map.145 = (f32[64,512]{1,0:T(8,128)}, bf16[64,256]{1,0:T(8,128)(2,1)}, f32[16,512]{1,0:T(8,128)}, f32[16,512]{1,0:T(8,128)}, f32[9,16,16]{2,1,0:T(8,128)}, /*index=5*/f32[9,16,16]{2,1,0:T(8,128)}, f32[1,16]{1,0:T(1,128)}) custom-call(f32[16]{0:T(128)} %head.1, f32[16,16,128]{2,1,0:T(8,128)} %get-tuple-element.17.fin, bf16[9,16,16]{2,1,0:T(8,128)(2,1)} %bitcast.18, ...), custom_call_target="tpu_custom_call" | custom-call | tf_op jit(solution)/shard_map/pallas_call | solution.py:575

commit v8 on v7

--- a/solution.py
+++ b/solution.py
@@ -99,11 +99,12 @@
     lane = ids((16, LANES), 1)
 
     barrier = pltpu.get_barrier_semaphore()
-    sources = [(hop(me, d), half) for d in range(1, BEHIND + 1)]
-    sources += [(hop(me, -d), half) for d in range(1, REACH + 1)]
+    far_first = sorted(range(1, PLANES), key=lambda s: -min(s, PLANES - s))
+    sources = [(lax.rem(plane + s, PLANES) * GROUP + place, half) for s in far_first]
+    sources += [(hop(me, d), half) for d in range(BEHIND, 0, -1)]
+    sources += [(hop(me, -d), half) for d in range(REACH, 0, -1)]
+    sources += [(me, other)]
     sources += [(base + lax.rem(place + s, GROUP), half) for s in range(1, GROUP)]
-    sources += [(lax.rem(plane + s, PLANES) * GROUP + place, half) for s in range(1, PLANES)]
-    sources += [(me, other)]
     for chrom, chan in sources:
         pl.semaphore_signal(
             barrier, inc=1, device_id={"chrom": chrom, "chan": chan}, device_id_type=MESH
@@ -231,18 +232,24 @@
     def pair_row(q):
         left = lcol[q]
         limits = [edge[t, pl.ds(q, 1), :] for t in range(TILES)]
-        for e in range(-2, 3):
+        for e in range(-2, 2):
             move = e * d1
+            tiles = []
             for t in range(TILES):
                 mask = lane < limits[t] - move
                 if e < 0 and t == 0:
                     mask = mask & (lane >= -move)
                 value = left * band[q + RIM + move, :, cols(t)]
-                px[e + 2, q, :, cols(t)] = jnp.where(mask, value, 0.0).astype(BF16)
+                tiles.append(jnp.where(mask, value, 0.0).astype(BF16))
+                px[e + 2, q, :, cols(t)] = tiles[t]
+            if e == 0:
+                centre = tiles
+        for t, tile in enumerate(shift_tiles(centre, -2, d1)):
+            px[4, q, :, cols(t)] = tile
 
     def first_band_rows(s, _):
-        for u in range(BATCH):
-            band_row(s * BATCH + u)
+        for u in range(20):
+            band_row(s * 20 + u)
         return 0
 
     def pair_rows(s, _):
@@ -251,7 +258,7 @@
             band_row(2 * RIM + (s + 1) * BATCH + u)
         return 0
 
-    lax.fori_loop(0, 2 * RIM // BATCH + 1, first_band_rows, 0)
+    lax.fori_loop(0, (2 * RIM + BATCH) // 20, first_band_rows, 0)
     lax.fori_loop(0, SLAB // BATCH, pair_rows, 0)
 
     def tap_rows(q):
@@ -438,7 +445,7 @@
             device_id={"chrom": target * GROUP + place, "chan": half}, device_id_type=MESH,
         )
 
-    planes = [(s, lax.rem(plane + s, PLANES)) for s in range(1, PLANES)]
+    planes = [(s, lax.rem(plane + s, PLANES)) for s in far_first]
     for s, p in planes:
         plane_copy(s, plane, p).start()
 

time: 52.7 us -> 52 us (0.987)
  Pallas kernels: 52 us -> 51.3 us
    pallas_call x1, Pallas kernels: 50 us -> 49.3 us  [band_call(): pl.pallas_call(functools.partial(band_kernel, scale), out_shape=(jax.Shap...]
where the time goes in v8:
time: 52 us; the launch traced here: 51.9 us
  Pallas kernels  51.3 us (99%)
  between operations  0.64 us (1%)
    pallas_call x1, Pallas kernels, band_call(): pl.pallas_call(functools.partial(band_kernel, scale), out_shape=(jax.Shap...  49.3 us
    pallas_call x1, Pallas kernels, output_call(): pl.pallas_call(output_kernel, out_shape=(jax.ShapeDtypeStruct((ROWS, OFF)...  1.94 us

profile of v8, /device:TPU:1, one launch (start us, length us, event | category | flops | bytes accessed | tf_op | source)
XLA Modules:
  0.0 51.9 jit_solution(8530916473821735338)
XLA Ops:
  0.6 49.3 %shard_map.144 = (f32[64,512]{1,0:T(8,128)}, bf16[64,256]{1,0:T(8,128)(2,1)}, f32[16,16,128]{2,1,0:T(8,128)}) custom-call(s32[8]{0:T(128)} %ends_in.1, s32[2]{0:T(128)} %dil_in.1, f32[16]{0:T(128)} %head.1, bf16[64,256]{1,0:T(8,128)(2,1)} %emb.1, bf16[16,512]{1,0:T(8,128)(2,1)} %bitcast.20, bf16[16,512]{1,0:T(8,128)(2,1)} %bitcast.21, ...), custom_call_target="tpu_custom_call" | custom-call | tf_op jit(solution)/shard_map/pallas_call | solution.py:488
  50.0 1.9 %shard_map.145 = (f32[64,512]{1,0:T(8,128)}, bf16[64,256]{1,0:T(8,128)(2,1)}, f32[16,512]{1,0:T(8,128)}, f32[16,512]{1,0:T(8,128)}, f32[9,16,16]{2,1,0:T(8,128)}, /*index=5*/f32[9,16,16]{2,1,0:T(8,128)}, f32[1,16]{1,0:T(1,128)}) custom-call(f32[16]{0:T(128)} %head.1, f32[16,16,128]{2,1,0:T(8,128)} %get-tuple-element.17.fin, bf16[9,16,16]{2,1,0:T(8,128)(2,1)} %bitcast.18, ...), custom_call_target="tpu_custom_call" | custom-call | tf_op jit(solution)/shard_map/pallas_call | solution.py:582
